TPU v7x, 256 devices: a whole 4x4x8 slice. The times are simulated.
256 devices in a mesh: tile: 32 (over y, x, core), lev: 8 (over z).
Axes of the slice: x: 4, y: 4, z: 8, core: 2. Of those that a mesh axis runs over, the one named last changes fastest.
Arguments:
- conc: float32 [3, 48, 1024, 384], P(None, 'lev', 'tile'), may hold values from -6 to 6
- u_wind: float32 [48, 1024, 384], P('lev', 'tile'), may hold values from -0.15 to 0.15
- v_wind: float32 [48, 1024, 384], P('lev', 'tile'), may hold values from -0.15 to 0.15
- mixing: float32 [48, 1024, 384], P('lev', 'tile'), may hold values from 0.02 to 0.2
- kernels: float32 [8, 48], P(None, 'lev'), may hold values from 0.02 to 0.3
- observed: float32 [3, 32768], P(None, 'tile'), may hold values from -6 to 6
- obs_weight: float32 [32768], P('tile'), may hold values from 1 to 16
- column_tile: int32 [32768, 1], P('tile'), may hold values from 0 to 31; in each aligned block of 1024 rows (0 to 1023, 1024 to 2047, ...) at most 64 rows name the same one
- footprint: int32 [32768, 4], P('tile'), may hold values from 0 to 12287
- kernel_index: int32 [32768], P('tile'), may hold values from 0 to 7
Outputs:
- residual: float32 [3, 32768], P(None, 'tile')
- gradient: float32 [3, 48, 1024, 384], P(None, 'lev', 'tile')
Inputs may be any that keep to these rules, and one draw needn't show every extreme that they name: `column_tile`: among the 1024 soundings of one tile, no column tile is named more than 64 times, and some column tile is named exactly 64 times. A footprint column is a longitude offset times 384 plus a latitude within the column tile.
All inputs are finite; a program needn't handle non-finite values.
Results may differ from a plain program's by a relative error of at most 0.00014.
Values sent between devices are 32-bit elements; how exact they have to be, the bound alone decides.
A program may use at most 192 MiB of HBM per device.

v0:
```python
import jax
import jax.numpy as jnp
from jax import lax
from jax.sharding import PartitionSpec as P


def shifted(block, axis, distance):
    devices = range(lax.axis_size(axis))
    route = [(i - distance, i) for i in devices if i - distance in devices]
    return lax.ppermute(block, axis, route)


def padded_2(x, sides, width):
    for axis, dim in sides:
        devices, length = (lax.axis_size(axis), x.shape[dim])
        up = [(i, (i + 1) % devices) for i in range(devices - 1)]
        down = [(j, i) for i, j in up]
        last = lax.slice_in_dim(x, length - width, length, axis=dim)
        leading = lax.slice_in_dim(x, 0, width, axis=dim)
        before = lax.ppermute(last, axis, up)
        after = lax.ppermute(leading, axis, down)
        x = jnp.concatenate([before, x, after], axis=dim)
    return x


def shift_north(values):
    return jnp.concatenate([values[..., 1:], jnp.zeros_like(values[..., :1])], -1)


def shift_south(values):
    return jnp.concatenate([jnp.zeros_like(values[..., :1]), values[..., :-1]], -1)


def face_parts(tracer_field, winds):
    centre = tracer_field[..., 1:-1, 1:-1, :]
    east_cell = tracer_field[..., 1:-1, 2:, :]
    west_cell = tracer_field[..., 1:-1, :-2, :]
    upper_cell = tracer_field[..., 2:, 1:-1, :]
    lower_cell = tracer_field[..., :-2, 1:-1, :]
    open_face = (jnp.arange(tracer_field.shape[-1]) < tracer_field.shape[-1] - 1).astype(
        jnp.float32
    )
    u_centre = winds[0, 1:-1, 1:-1, :]
    u_west = winds[0, 1:-1, :-2, :]
    v_centre = winds[1, 1:-1, 1:-1, :] * open_face
    k_centre = winds[2, 1:-1, 1:-1, :]
    k_lower = winds[2, :-2, 1:-1, :]
    vertical = k_centre * (upper_cell - centre) - k_lower * (centre - lower_cell)
    return (centre, east_cell, west_cell, u_centre, u_west, v_centre, vertical)


def advance(tracer_field, winds):
    centre, east_cell, west_cell, u_centre, u_west, v_centre, vertical = face_parts(
        tracer_field, winds
    )
    flux_east = jnp.maximum(u_centre, 0.0) * centre + jnp.minimum(u_centre, 0.0) * east_cell
    flux_west = jnp.maximum(u_west, 0.0) * west_cell + jnp.minimum(u_west, 0.0) * centre
    flux_north = jnp.maximum(v_centre, 0.0) * centre + jnp.minimum(v_centre, 0.0) * shift_north(
        centre
    )
    return centre - flux_east + flux_west - flux_north + shift_south(flux_north) + vertical


def adjoint(tracer_field, winds):
    centre, east_cell, west_cell, u_centre, u_west, v_centre, vertical = face_parts(
        tracer_field, winds
    )
    along_lon = jnp.maximum(u_centre, 0.0) * (east_cell - centre) + jnp.minimum(u_west, 0.0) * (
        centre - west_cell
    )
    along_lat = jnp.maximum(v_centre, 0.0) * (shift_north(centre) - centre) + shift_south(
        jnp.minimum(v_centre, 0.0)
    ) * (centre - shift_south(centre))
    return centre + along_lon + along_lat + vertical


def body(
    conc,
    u_wind,
    v_wind,
    mixing,
    kernels,
    observed,
    obs_weight,
    column_tile,
    footprint,
    kernel_index,
):
    tile_count = lax.axis_size("tile")
    lev_dev, lon_dev, lat_count = u_wind.shape
    snd_count = footprint.shape[0]
    foot_count = footprint.shape[1]
    kind_count = kernels.shape[0]
    tracer_count = conc.shape[0]
    col_count = lon_dev * lat_count
    capacity = 2 * snd_count // tile_count
    slot_count = capacity * tile_count
    stacked = jnp.stack((u_wind, v_wind, mixing))
    west_col = shifted(stacked[:, :, -1:, :], "tile", 1)
    below_row = shifted(stacked[:, -1:, :, :], "lev", 1)
    side_zero = jnp.zeros((3, lev_dev, 1, lat_count), jnp.float32)
    middle = jnp.concatenate([west_col, stacked, side_zero], 2)
    corner_zero = jnp.zeros((3, 1, 1, lat_count), jnp.float32)
    bottom = jnp.concatenate([corner_zero, below_row, corner_zero], 2)
    top_zero = jnp.zeros((3, 1, lon_dev + 2, lat_count), jnp.float32)
    wind_ext = jnp.concatenate([bottom, middle, top_zero], 1)

    def evolve(tracer_field, stepper):
        current = tracer_field
        for sweep_index in range(2):
            padded = padded_2(current, (("tile", 2), ("lev", 1)), 1)
            current = stepper(padded, wind_ext)
        return current

    evolved = evolve(conc, advance)
    target = column_tile[:, 0]
    matches = (target[:, None] == jnp.arange(tile_count)[None, :]).astype(jnp.int32)
    slot_rank = jnp.sum((jnp.cumsum(matches, 0) - matches) * matches, 1)
    placed = target * capacity + slot_rank
    indices = jnp.concatenate([footprint.T, kernel_index[None, :]], 0)
    packed_ids = jnp.zeros((foot_count + 1, slot_count), jnp.int32).at[:, placed].set(indices)
    ids_in = lax.all_to_all(packed_ids, "tile", split_axis=1, concat_axis=1, tiled=True)
    foot_in = ids_in[:foot_count]
    kind_in = ids_in[foot_count]
    columns_flat = evolved.reshape(tracer_count, lev_dev, col_count)
    profile_sums = jnp.einsum("kl,tlc->tkc", kernels, columns_flat, precision=lax.Precision.HIGHEST)
    profile_flat = profile_sums.reshape(tracer_count, kind_count * col_count)
    flat_index = kind_in[None, :] * col_count + foot_in
    picked = jnp.take(profile_flat, flat_index.reshape(-1), axis=1).reshape(
        tracer_count, foot_count, slot_count
    )
    partial_value = jnp.sum(picked, 1)
    model_in = lax.psum(partial_value, "lev") / foot_count
    model_back = lax.all_to_all(model_in, "tile", split_axis=1, concat_axis=1, tiled=True)
    residual = model_back[:, placed] - observed
    weighted = obs_weight[None, :] * residual / foot_count
    packed_weighted = jnp.zeros((tracer_count, slot_count), jnp.float32).at[:, placed].set(weighted)
    weighted_in = lax.all_to_all(packed_weighted, "tile", split_axis=1, concat_axis=1, tiled=True)
    foot_in = ids_in[:foot_count]
    kind_in = ids_in[foot_count]
    flat_index = kind_in[None, :] * col_count + foot_in
    term_rows = jnp.broadcast_to(
        weighted_in[:, None, :], (tracer_count, foot_count, slot_count)
    ).reshape(tracer_count, -1)
    summed = (
        jnp.zeros((tracer_count, kind_count * col_count), jnp.float32)
        .at[:, flat_index.reshape(-1)]
        .add(term_rows)
    )
    forcing = jnp.einsum(
        "kl,tkc->tlc",
        kernels,
        summed.reshape(tracer_count, kind_count, col_count),
        precision=lax.Precision.HIGHEST,
    )
    forcing = forcing.reshape(tracer_count, lev_dev, lon_dev, lat_count)
    gradient = evolve(forcing, adjoint)
    return (residual, gradient)


def solution(mesh):
    placed = (
        P(None, "lev", "tile", None),
        P("lev", "tile", None),
        P("lev", "tile", None),
        P("lev", "tile", None),
        P(None, "lev"),
        P(None, "tile"),
        P("tile"),
        P("tile", None),
        P("tile", None),
        P("tile"),
    )
    return jax.shard_map(
        body,
        mesh=mesh,
        in_specs=placed,
        out_specs=(P(None, "tile"), P(None, "lev", "tile", None)),
        check_vma=False,
    )
```

profile of v0, /device:TPU:1, one launch (start us, length us, event | category | flops | bytes accessed | tf_op | source)
XLA Modules:
  0.0 369.8 jit_solution(2450955228281779693)
XLA Ops:
  2.3 5.0 %collective-permute-start.4 = (f32[3,1,32,384]{3,2,1,0:T(8,128)}, f32[3,1,32,384]{3,2,1,0:T(8,128)}, u32[]{:S(2)}, u32[]{:S(2)}) collective-permute-start(f32[3,1,32,384]{3,2,1,0:T(8,128)} %pad_maximum_fusion.52), channel_id=1, source_target_pairs={{0,1},{1,2},{2,3},{3,4},{4,5},{5,6},{6,7},{8,9},{9,10},{10,11},{11... | collective-permute-start | bytes 442376 | tf_op jit(solution)/shard_map/ppermute | solution.py:10
  8.9 3.9 %collective-permute-start.1 = (f32[3,6,1,384]{3,2,1,0:T(1,128)}, f32[3,6,1,384]{3,2,1,0:T(1,128)}, u32[]{:S(2)}, u32[]{:S(2)}) collective-permute-start(f32[3,6,1,384]{3,2,1,0:T(1,128)} %pad_maximum_fusion.54), channel_id=1, source_target_pairs={{0,8},{8,16},{16,24},{24,32},{32,40},{40,48},{48,56},{56,64},{64,7... | collective-permute-start | bytes 82952 | tf_op jit(solution)/shard_map/ppermute | solution.py:10
  16.5 3.6 collective-permute-start.2
  20.9 9.0 %reduce-window.6 = s32[32,8,128]{2,1,0:T(8,128)S(1)} reduce-window(s32[32,8,128]{2,1,0:T(8,128)S(1)} %fusion.71, s32[]{:T(128)} %constant.11.clone.1), window={size=1x1x128 pad=0_0x0_0x127_0}, to_apply=%region_0.0 | reduce-window | flops 4161536 | bytes 262148 | tf_op jit(solution)/shard_map/reduce-window
  32.7 4.1 %scatter_custom_fusion = s32[5,2048]{0,1:T(8,128)} fusion(s32[1024]{0:T(1024)S(1)} %bitcast.118, s32[1024,5]{1,0:T(8,128)S(1)} %copy.75, s32[]{:T(128)} %constant.11.clone.1), kind=kCustom, calls=%fused_computation.104 | custom fusion | bytes 40964 | tf_op jit(solution)/shard_map/scatter | solution.py:121
  39.2 8.8 %all-to-all-start = ((s32[32,1,320]{2,1,0:T(1,128)}), s32[32,1,320]{2,1,0:T(1,128)}, u32[]{:S(2)}, u32[]{:S(2)}) async-start(s32[32,1,320]{2,1,0:T(1,128)} %reshape.177), calls=%async_computation | async-start | bytes 98304 | tf_op jit(solution)/shard_map/all_to_all | solution.py:122
  52.3 4.7 %collective-permute-start.5 = (f32[3,1,34,384]{3,2,1,0:T(8,128)}, f32[3,1,34,384]{3,2,1,0:T(8,128)}, u32[]{:S(2)}, u32[]{:S(2)}) collective-permute-start(f32[3,1,34,384]{3,2,1,0:T(8,128)} %get-tuple-element.23), channel_id=1, source_target_pairs={{0,1},{1,2},{2,3},{3,4},{4,5},{5,6},{6,7},{8,9},{9,10},{10,11},{11... | collective-permute-start | bytes 470024 | tf_op jit(solution)/shard_map/ppermute | solution.py:20
  62.8 2.9 collective-permute-start.6
  65.7 3.3 collective-permute-start.7
  71.3 4.6 %collective-permute-start.9 = (f32[3,1,34,384]{3,2,1,0:T(8,128)S(1)}, f32[3,1,34,384]{3,2,1,0:T(8,128)S(1)}, u32[]{:S(2)}, u32[]{:S(2)}) collective-permute-start(f32[3,1,34,384]{3,2,1,0:T(8,128)S(1)} %get-tuple-element.21), channel_id=1, source_target_pairs={{0,1},{1,2},{2,3},{3,4},{4,5},{5,6},{6,7},{8,9},{9,10},{10,11},{11... | collective-permute-start | bytes 470024 | tf_op jit(solution)/shard_map/ppermute | solution.py:20
  81.9 2.4 convolution_bitcast_fusion.1
  84.3 23.6 %copy.91 = f32[3,8,12288]{0,2,1:T(8,128)} copy(f32[3,8,12288]{2,1,0:T(8,128)S(1)} %convolution_bitcast_fusion.1) | data formatting | bytes 2359296 | tf_op jit(solution)/shard_map/reshape | solution.py:127
  107.9 43.3 %gather_fusion = f32[8192,3]{1,0:T(8,128)} fusion(f32[3,98304]{0,1:T(8,128)} %bitcast.84, s32[8192]{0:T(1024)S(1)} %broadcast_clamp_fusion), kind=kCustom, calls=%fused_computation | custom fusion | bytes 229376 | tf_op jit(solution)/shard_map/jit(_take)/gather | solution.py:129
  151.2 3.7 select_reduce_fusion
  155.2 27.5 %psum.7 = f32[3,2048]{1,0:T(4,128)S(1)} all-reduce(f32[3,2048]{1,0:T(4,128)S(1)} %copy.80), channel_id=1, replica_groups=mesh['tile'=32,'lev'=8] {'lev'}, use_global_device_ids=true, to_apply=%region_5.6 | all-reduce | flops 6144 | bytes 49152 | tf_op jit(solution)/shard_map/psum | solution.py:133
  183.6 15.8 %all-to-all-start.1 = ((f32[32,1,192]{2,1,0:T(1,128)}), f32[32,1,192]{2,1,0:T(1,128)S(1)}, u32[]{:S(2)}, u32[]{:S(2)}) async-start(f32[32,1,192]{2,1,0:T(1,128)} %reshape.179), calls=%async_computation.1 | async-start | bytes 65536 | tf_op jit(solution)/shard_map/all_to_all | solution.py:134
  199.6 7.0 %all-to-all-done.1 = f32[32,1,192]{2,1,0:T(1,128)S(1)} async-done(((f32[32,1,192]{2,1,0:T(1,128)}), f32[32,1,192]{2,1,0:T(1,128)S(1)}, u32[]{:S(2)}, u32[]{:S(2)}) %all-to-all-start.1) | async-done | bytes 24608 | tf_op jit(solution)/shard_map/all_to_all | solution.py:134
  209.3 4.0 %gather_fusion.1 = f32[1024,3]{1,0:T(8,128)S(1)} fusion(f32[3,2048]{0,1:T(8,128)} %bitcast.102, s32[1024]{0:T(1024)S(1)} %broadcast_clamp_fusion.1), kind=kCustom, calls=%fused_computation.1 | custom fusion | bytes 28672 | tf_op jit(solution)/shard_map/gather | solution.py:135
  213.4 3.9 %scatter_custom_fusion.1 = f32[3,2048]{0,1:T(8,128)S(1)} fusion(s32[1024]{0:T(1024)S(1)} %bitcast.120, f32[3,1024]{0,1:T(8,128)S(1)} %bitcast_subtract_fusion, f32[]{:T(128)} %constant.17.clone.1, f32[]{:T(128)} %constant.20.clone.1, f32[1024]{0:T(1024)S(1)} %copy-done.15), kind=kCustom, calls=%fused_computation.98 | custom fusion | flops 6144 | bytes 552968 | tf_op jit(solution)/shard_map/scatter | solution.py:137
  217.8 10.7 %all_to_all.30 = f32[32,1,192]{2,1,0:T(1,128)S(1)} all-to-all(f32[32,1,192]{2,1,0:T(1,128)S(1)} %reshape.181), channel_id=1, replica_groups=mesh['tile'=32,'lev'=8] {'tile'}, dimensions={0} | all-to-all | bytes 49152 | tf_op jit(solution)/shard_map/all_to_all | solution.py:138
  229.8 2.3 broadcast_in_dim.35
  232.1 69.1 %scatter_custom_fusion.2 = f32[3,98304]{0,1:T(8,128)} fusion(s32[8192]{0:T(1024)} %bitcast.112, f32[8192,3]{1,0:T(8,128)} %bitcast.98, f32[]{:T(128)} %constant.17.clone.1), kind=kCustom, calls=%fused_computation.5 | custom fusion | flops 24576 | bytes 1180160 | tf_op jit(solution)/shard_map/scatter-add | solution.py:148
  301.2 27.0 %copy.87 = f32[3,8,12288]{2,1,0:T(8,128)S(1)} copy(f32[3,8,12288]{0,2,1:T(8,128)} %bitcast.83) | data formatting | bytes 2359296 | tf_op jit(solution)/shard_map/reshape | solution.py:153
  328.2 2.2 convolution_bitcast_fusion
  332.1 3.2 collective-permute-start.10
  335.4 2.3 collective-permute-start.11
  340.0 4.0 %collective-permute-start.13 = (f32[3,1,34,384]{3,2,1,0:T(8,128)S(1)}, f32[3,1,34,384]{3,2,1,0:T(8,128)S(1)}, u32[]{:S(2)}, u32[]{:S(2)}) collective-permute-start(f32[3,1,34,384]{3,2,1,0:T(8,128)S(1)} %get-tuple-element.19), channel_id=1, source_target_pairs={{0,1},{1,2},{2,3},{3,4},{4,5},{5,6},{6,7},{8,9},{9,10},{10,11},{11... | collective-permute-start | bytes 470024 | tf_op jit(solution)/shard_map/ppermute | solution.py:20
  344.3 2.6 collective-permute-done.12
  348.7 3.1 collective-permute-start.14
  351.8 3.3 collective-permute-start.15
  358.4 4.7 %collective-permute-start.17 = (f32[3,1,34,384]{3,2,1,0:T(8,128)S(1)}, f32[3,1,34,384]{3,2,1,0:T(8,128)S(1)}, u32[]{:S(2)}, u32[]{:S(2)}) collective-permute-start(f32[3,1,34,384]{3,2,1,0:T(8,128)S(1)} %get-tuple-element.17), channel_id=1, source_target_pairs={{0,1},{1,2},{2,3},{3,4},{4,5},{5,6},{6,7},{8,9},{9,10},{10,11},{11... | collective-permute-start | bytes 470024 | tf_op jit(solution)/shard_map/ppermute | solution.py:20
  367.1 2.6 fusion.5
  (129 shorter events, 50.2 us)
Async XLA Ops:
  0.6 81.3 %copy-start = (f32[8,6]{1,0:T(8,128)S(1)}, f32[8,6]{1,0:T(8,128)}, u32[]{:S(2)}) copy-start(f32[8,6]{1,0:T(8,128)} %param.14) | copy-start | bytes 580
  0.6 47.7 %copy-start.5 = (f32[6,32,384]{2,1,0:T(8,128)S(1)}, f32[6,32,384]{2,1,0:T(8,128)}, u32[]{:S(2)}) copy-start(f32[6,32,384]{2,1,0:T(8,128)} %param.11) | copy-start | bytes 884740
  0.7 47.7 %copy-start.4 = (f32[6,32,384]{2,1,0:T(8,128)S(1)}, f32[6,32,384]{2,1,0:T(8,128)}, u32[]{:S(2)}) copy-start(f32[6,32,384]{2,1,0:T(8,128)} %param.12) | copy-start | bytes 884740
  0.7 47.3 %copy-start.1 = (f32[3,6,32,384]{3,2,1,0:T(8,128)S(1)}, f32[3,6,32,384]{3,2,1,0:T(8,128)}, u32[]{:S(2)}) copy-start(f32[3,6,32,384]{3,2,1,0:T(8,128)} %param.10) | copy-start | bytes 2654212
  2.3 57.2 %collective-permute-start.4 = (f32[3,1,32,384]{3,2,1,0:T(8,128)}, f32[3,1,32,384]{3,2,1,0:T(8,128)}, u32[]{:S(2)}, u32[]{:S(2)}) collective-permute-start(f32[3,1,32,384]{3,2,1,0:T(8,128)} %pad_maximum_fusion.52), channel_id=1, source_target_pairs={{0,1},{1,2},{2,3},{3,4},{4,5},{5,6},{6,7},{8,9},{9,10},{10,11},{11... | collective-permute-start | bytes 442376 | tf_op jit(solution)/shard_map/ppermute | solution.py:10
  8.9 50.6 %collective-permute-start.1 = (f32[3,6,1,384]{3,2,1,0:T(1,128)}, f32[3,6,1,384]{3,2,1,0:T(1,128)}, u32[]{:S(2)}, u32[]{:S(2)}) collective-permute-start(f32[3,6,1,384]{3,2,1,0:T(1,128)} %pad_maximum_fusion.54), channel_id=1, source_target_pairs={{0,8},{8,16},{16,24},{24,32},{32,40},{40,48},{48,56},{56,64},{64,7... | collective-permute-start | bytes 82952 | tf_op jit(solution)/shard_map/ppermute | solution.py:10
  14.6 34.9 %collective-permute-start = (f32[3,6,1,384]{3,2,1,0:T(1,128)}, f32[3,6,1,384]{3,2,1,0:T(1,128)}, u32[]{:S(2)}, u32[]{:S(2)}) collective-permute-start(f32[3,6,1,384]{3,2,1,0:T(1,128)} %get-tuple-element.36), channel_id=1, source_target_pairs={{8,0},{16,8},{24,16},{32,24},{40,32},{48,40},{56,48},{64,56},{72,6... | collective-permute-start | bytes 82952 | tf_op jit(solution)/shard_map/ppermute | solution.py:21
  16.5 33.0 %collective-permute-start.2 = (f32[3,6,1,384]{3,2,1,0:T(1,128)}, f32[3,6,1,384]{3,2,1,0:T(1,128)}, u32[]{:S(2)}, u32[]{:S(2)}) collective-permute-start(f32[3,6,1,384]{3,2,1,0:T(1,128)} %get-tuple-element.35), channel_id=1, source_target_pairs={{0,8},{8,16},{16,24},{24,32},{32,40},{40,48},{48,56},{56,64},{64,7... | collective-permute-start | bytes 82952 | tf_op jit(solution)/shard_map/ppermute | solution.py:20
  31.8 16.2 %copy-start.13 = (s32[1024,1]{0,1:T(1,128)}, s32[1024,1]{0,1:T(1,128)S(1)}, u32[]{:S(2)}) copy-start(s32[1024,1]{0,1:T(1,128)S(1)} %compare_select_fusion.2) | copy-start | bytes 12292
  39.2 17.8 %all-to-all-start = ((s32[32,1,320]{2,1,0:T(1,128)}), s32[32,1,320]{2,1,0:T(1,128)}, u32[]{:S(2)}, u32[]{:S(2)}) async-start(s32[32,1,320]{2,1,0:T(1,128)} %reshape.177), calls=%async_computation | async-start | bytes 98304 | tf_op jit(solution)/shard_map/all_to_all | solution.py:122
  48.0 11.6 %copy-start.2 = (f32[6,32,384]{2,1,0:T(8,128)S(1)}, f32[6,32,384]{2,1,0:T(8,128)}, u32[]{:S(2)}) copy-start(f32[6,32,384]{2,1,0:T(8,128)} %param.13) | copy-start | bytes 884740
  51.0 9.7 %collective-permute-start.3 = (f32[3,1,34,384]{3,2,1,0:T(8,128)}, f32[3,1,34,384]{3,2,1,0:T(8,128)}, u32[]{:S(2)}, u32[]{:S(2)}) collective-permute-start(f32[3,1,34,384]{3,2,1,0:T(8,128)} %get-tuple-element.22), channel_id=1, source_target_pairs={{1,0},{2,1},{3,2},{4,3},{5,4},{6,5},{7,6},{9,8},{10,9},{11,10},{12... | collective-permute-start | bytes 470024 | tf_op jit(solution)/shard_map/ppermute | solution.py:21
  52.3 8.4 %collective-permute-start.5 = (f32[3,1,34,384]{3,2,1,0:T(8,128)}, f32[3,1,34,384]{3,2,1,0:T(8,128)}, u32[]{:S(2)}, u32[]{:S(2)}) collective-permute-start(f32[3,1,34,384]{3,2,1,0:T(8,128)} %get-tuple-element.23), channel_id=1, source_target_pairs={{0,1},{1,2},{2,3},{3,4},{4,5},{5,6},{6,7},{8,9},{9,10},{10,11},{11... | collective-permute-start | bytes 470024 | tf_op jit(solution)/shard_map/ppermute | solution.py:20
  62.7 17.1 %copy-start.6 = (f32[6,32,384]{2,1,0:T(8,128)S(1)}, f32[6,32,384]{2,1,0:T(8,128)}, u32[]{:S(2)}) copy-start(f32[6,32,384]{2,1,0:T(8,128)} %get-tuple-element.41) | copy-start | bytes 884740
  62.8 6.5 %collective-permute-start.6 = (f32[3,6,1,384]{3,2,1,0:T(1,128)S(1)}, f32[3,6,1,384]{3,2,1,0:T(1,128)S(1)}, u32[]{:S(2)}, u32[]{:S(2)}) collective-permute-start(f32[3,6,1,384]{3,2,1,0:T(1,128)S(1)} %get-tuple-element.34), channel_id=1, source_target_pairs={{8,0},{16,8},{24,16},{32,24},{40,32},{48,40},{56,48},{64,56},{72,6... | collective-permute-start | bytes 82952 | tf_op jit(solution)/shard_map/ppermute | solution.py:21
  65.7 4.2 %collective-permute-start.7 = (f32[3,6,1,384]{3,2,1,0:T(1,128)S(1)}, f32[3,6,1,384]{3,2,1,0:T(1,128)S(1)}, u32[]{:S(2)}, u32[]{:S(2)}) collective-permute-start(f32[3,6,1,384]{3,2,1,0:T(1,128)S(1)} %get-tuple-element.33), channel_id=1, source_target_pairs={{0,8},{8,16},{16,24},{24,32},{32,40},{40,48},{48,56},{56,64},{64,7... | collective-permute-start | bytes 82952 | tf_op jit(solution)/shard_map/ppermute | solution.py:20
  70.0 8.1 %collective-permute-start.8 = (f32[3,1,34,384]{3,2,1,0:T(8,128)S(1)}, f32[3,1,34,384]{3,2,1,0:T(8,128)S(1)}, u32[]{:S(2)}, u32[]{:S(2)}) collective-permute-start(f32[3,1,34,384]{3,2,1,0:T(8,128)S(1)} %get-tuple-element.20), channel_id=1, source_target_pairs={{1,0},{2,1},{3,2},{4,3},{5,4},{6,5},{7,6},{9,8},{10,9},{11,10},{12... | collective-permute-start | bytes 470024 | tf_op jit(solution)/shard_map/ppermute | solution.py:21
  71.3 8.6 %collective-permute-start.9 = (f32[3,1,34,384]{3,2,1,0:T(8,128)S(1)}, f32[3,1,34,384]{3,2,1,0:T(8,128)S(1)}, u32[]{:S(2)}, u32[]{:S(2)}) collective-permute-start(f32[3,1,34,384]{3,2,1,0:T(8,128)S(1)} %get-tuple-element.21), channel_id=1, source_target_pairs={{0,1},{1,2},{2,3},{3,4},{4,5},{5,6},{6,7},{8,9},{9,10},{10,11},{11... | collective-permute-start | bytes 470024 | tf_op jit(solution)/shard_map/ppermute | solution.py:20
  107.9 91.4 %copy-start.14 = (s32[1024,1]{0,1:T(1,128)S(1)}, s32[1024,1]{0,1:T(1,128)}, u32[]{:S(2)}) copy-start(s32[1024,1]{0,1:T(1,128)} %copy-done.13) | copy-start | bytes 12292
  107.9 91.5 %copy-start.12 = (f32[3,1024]{1,0:T(4,128)S(1)}, f32[3,1024]{1,0:T(4,128)}, u32[]{:S(2)}) copy-start(f32[3,1024]{1,0:T(4,128)} %param.15) | copy-start | bytes 36868
  151.2 62.2 %copy-start.15 = (f32[1024]{0:T(1024)S(1)}, f32[1024]{0:T(1024)}, u32[]{:S(2)}) copy-start(f32[1024]{0:T(1024)} %param.16) | copy-start | bytes 12292
  183.6 23.0 %all-to-all-start.1 = ((f32[32,1,192]{2,1,0:T(1,128)}), f32[32,1,192]{2,1,0:T(1,128)S(1)}, u32[]{:S(2)}, u32[]{:S(2)}) async-start(f32[32,1,192]{2,1,0:T(1,128)} %reshape.179), calls=%async_computation.1 | async-start | bytes 65536 | tf_op jit(solution)/shard_map/all_to_all | solution.py:134
  213.4 18.7 %copy-start.3 = (f32[3,1024]{0,1:T(8,128)}, f32[3,1024]{0,1:T(8,128)S(1)}, u32[]{:S(2)}) copy-start(f32[3,1024]{0,1:T(8,128)S(1)} %bitcast_subtract_fusion) | copy-start | bytes 36868
  332.1 5.7 %collective-permute-start.10 = (f32[3,6,1,384]{3,2,1,0:T(1,128)S(1)}, f32[3,6,1,384]{3,2,1,0:T(1,128)S(1)}, u32[]{:S(2)}, u32[]{:S(2)}) collective-permute-start(f32[3,6,1,384]{3,2,1,0:T(1,128)S(1)} %get-tuple-element.32), channel_id=1, source_target_pairs={{8,0},{16,8},{24,16},{32,24},{40,32},{48,40},{56,48},{64,56},{72,6... | collective-permute-start | bytes 82952 | tf_op jit(solution)/shard_map/ppermute | solution.py:21
  335.4 3.3 collective-permute-start.11
  338.7 8.2 %collective-permute-start.12 = (f32[3,1,34,384]{3,2,1,0:T(8,128)S(1)}, f32[3,1,34,384]{3,2,1,0:T(8,128)S(1)}, u32[]{:S(2)}, u32[]{:S(2)}) collective-permute-start(f32[3,1,34,384]{3,2,1,0:T(8,128)S(1)} %get-tuple-element.18), channel_id=1, source_target_pairs={{1,0},{2,1},{3,2},{4,3},{5,4},{6,5},{7,6},{9,8},{10,9},{11,10},{12... | collective-permute-start | bytes 470024 | tf_op jit(solution)/shard_map/ppermute | solution.py:21
  340.0 7.8 %collective-permute-start.13 = (f32[3,1,34,384]{3,2,1,0:T(8,128)S(1)}, f32[3,1,34,384]{3,2,1,0:T(8,128)S(1)}, u32[]{:S(2)}, u32[]{:S(2)}) collective-permute-start(f32[3,1,34,384]{3,2,1,0:T(8,128)S(1)} %get-tuple-element.19), channel_id=1, source_target_pairs={{0,1},{1,2},{2,3},{3,4},{4,5},{5,6},{6,7},{8,9},{9,10},{10,11},{11... | collective-permute-start | bytes 470024 | tf_op jit(solution)/shard_map/ppermute | solution.py:20
  348.7 18.4 %copy-start.8 = (f32[6,32,384]{2,1,0:T(8,128)S(1)}, f32[6,32,384]{2,1,0:T(8,128)}, u32[]{:S(2)}) copy-start(f32[6,32,384]{2,1,0:T(8,128)} %copy-done.7) | copy-start | bytes 884740
  348.7 8.3 %collective-permute-start.14 = (f32[3,6,1,384]{3,2,1,0:T(1,128)S(1)}, f32[3,6,1,384]{3,2,1,0:T(1,128)S(1)}, u32[]{:S(2)}, u32[]{:S(2)}) collective-permute-start(f32[3,6,1,384]{3,2,1,0:T(1,128)S(1)} %get-tuple-element.28), channel_id=1, source_target_pairs={{8,0},{16,8},{24,16},{32,24},{40,32},{48,40},{56,48},{64,56},{72,6... | collective-permute-start | bytes 82952 | tf_op jit(solution)/shard_map/ppermute | solution.py:21
  351.8 5.2 %collective-permute-start.15 = (f32[3,6,1,384]{3,2,1,0:T(1,128)S(1)}, f32[3,6,1,384]{3,2,1,0:T(1,128)S(1)}, u32[]{:S(2)}, u32[]{:S(2)}) collective-permute-start(f32[3,6,1,384]{3,2,1,0:T(1,128)S(1)} %get-tuple-element.27), channel_id=1, source_target_pairs={{0,8},{8,16},{16,24},{24,32},{32,40},{40,48},{48,56},{56,64},{64,7... | collective-permute-start | bytes 82952 | tf_op jit(solution)/shard_map/ppermute | solution.py:20
  357.0 8.3 %collective-permute-start.16 = (f32[3,1,34,384]{3,2,1,0:T(8,128)S(1)}, f32[3,1,34,384]{3,2,1,0:T(8,128)S(1)}, u32[]{:S(2)}, u32[]{:S(2)}) collective-permute-start(f32[3,1,34,384]{3,2,1,0:T(8,128)S(1)} %get-tuple-element.16), channel_id=1, source_target_pairs={{1,0},{2,1},{3,2},{4,3},{5,4},{6,5},{7,6},{9,8},{10,9},{11,10},{12... | collective-permute-start | bytes 470024 | tf_op jit(solution)/shard_map/ppermute | solution.py:21
  358.4 8.8 %collective-permute-start.17 = (f32[3,1,34,384]{3,2,1,0:T(8,128)S(1)}, f32[3,1,34,384]{3,2,1,0:T(8,128)S(1)}, u32[]{:S(2)}, u32[]{:S(2)}) collective-permute-start(f32[3,1,34,384]{3,2,1,0:T(8,128)S(1)} %get-tuple-element.17), channel_id=1, source_target_pairs={{0,1},{1,2},{2,3},{3,4},{4,5},{5,6},{6,7},{8,9},{9,10},{10,11},{11... | collective-permute-start | bytes 470024 | tf_op jit(solution)/shard_map/ppermute | solution.py:20
  (4 other events, 23.0 us)
where the time goes:
time: 373 us; the launch traced here: 370 us
  local copies, waits for them, and re-layouts  121 us (32%)
  other arithmetic  105 us (28%)
  starting transfers between devices  80.3 us (22%)
  blocking collectives  38.2 us (10%)
  waiting for transfers between devices  19.3 us (5%)
  matrix products  4.55 us (1%)
    scatter-add x1, other arithmetic, body(): summed = jnp.zeros((tracer_count, kind_count * col_count), jnp.float32).a...  69.1 us
    gather x1, local copies, waits for them, and re-layouts, body(): jnp.take(profile_flat, flat_index.reshape(-1), axis=1)  43.3 us
    ppermute x8, starting transfers between devices, padded_2(): before = lax.ppermute(last, axis, up)  30.5 us
    psum x1, blocking collectives, body(): model_in = lax.psum(partial_value, 'lev') / foot_count  27.5 us
    reshape x1, local copies, waits for them, and re-layouts, body(): summed.reshape(tracer_count, kind_count, col_count)  27 us
    reshape x1, local copies, waits for them, and re-layouts, body(): profile_flat = profile_sums.reshape(tracer_count, kind_count * col_count)  23.6 us
    ppermute x8, starting transfers between devices, padded_2(): after = lax.ppermute(leading, axis, down)  16.3 us
    all_to_all x1, starting transfers between devices, body(): lax.all_to_all(model_in, 'tile', split_axis=1, concat_axis=1, tiled=True)  15.8 us
  transfers between devices with their start and end apart: 20, of which 9 were waited for; matrix products, arithmetic and copies ran while one was open for 9% of the time, Pallas kernels for 0%

commit v1 on v0

v1 whole, which is shorter than its diff:
```python
import functools

import jax
import jax.numpy as jnp
from jax import lax
from jax.experimental import pallas as pl
from jax.experimental.pallas import tpu as pltpu
from jax.sharding import PartitionSpec as P

MESH = pl.DeviceIdType.MESH
F32, BF16 = jnp.float32, jnp.bfloat16
NT = (((1,), (1,)), ((), ()))
TR, LV, LON, LAT = 3, 6, 32, 384
ROWS = TR * LV * LON
NTILE, NLEV, CAP, SND, FOOT = 32, 8, 64, 1024, 4
SLOTS = NTILE * CAP
CHUNK = SLOTS // NLEV
LOOK = FOOT * CHUNK


def parts_of(x, count):
    pieces = []
    for _ in range(count):
        piece = x.astype(BF16)
        pieces.append(piece)
        x = x - piece.astype(F32)
    return pieces


def kernel(
    conc, u_in, v_in, k_in, kern, fields,
    residual, gradient,
    x0, x1, x2, x3, u, v, k, lon_out, lon_in,
    ids_out, ids_in, hot, fa, fb, kw, lathot, lonhot, spread,
    e, picked, part_out, part_in, res, ret_in, terms, total,
    local_sem, halo_ss, halo_rs, ids_ss, ids_rs, part_ss, part_rs, res_ss, res_rs, ret_ss, ret_rs,
):
    tile, lev = lax.axis_index("tile"), lax.axis_index("lev")
    east, west = lax.rem(tile + 1, NTILE), lax.rem(tile + NTILE - 1, NTILE)
    above, below = lax.rem(lev + 1, NLEV), lax.rem(lev + NLEV - 1, NLEV)

    def remote(src, dst, ss, rs, target):
        return pltpu.make_async_remote_copy(
            src_ref=src, dst_ref=dst, send_sem=ss, recv_sem=rs, device_id=target, device_id_type=MESH
        )

    barrier = pltpu.get_barrier_semaphore()

    def greet_tile(d, carry):
        pl.semaphore_signal(
            barrier, inc=1, device_id={"tile": lax.rem(tile + d, NTILE)}, device_id_type=MESH
        )
        return carry

    def greet_lev(d, carry):
        pl.semaphore_signal(
            barrier, inc=1, device_id={"lev": lax.rem(lev + d, NLEV)}, device_id_type=MESH
        )
        return carry

    lax.fori_loop(1, NTILE, greet_tile, 0)
    lax.fori_loop(1, NLEV, greet_lev, 0)
    loads = [
        pltpu.make_async_copy(conc, x0.at[:, pl.ds(1, LV)], local_sem.at[0]),
        pltpu.make_async_copy(u_in, u, local_sem.at[1]),
        pltpu.make_async_copy(v_in, v, local_sem.at[2]),
        pltpu.make_async_copy(k_in, k.at[pl.ds(1, LV)], local_sem.at[3]),
    ]
    for copy in loads:
        copy.start()

    row8 = lax.broadcasted_iota(jnp.int32, (8, 128), 1) < CAP

    def lev_copies(x, i):
        return [
            remote(x.at[:, LV], x.at[:, 0], halo_ss.at[i, 0], halo_rs.at[i, 0], {"lev": above}),
            remote(x.at[:, 1], x.at[:, LV + 1], halo_ss.at[i, 1], halo_rs.at[i, 1], {"lev": below}),
        ]

    def lon_copies(i):
        return [
            remote(lon_out.at[i, 0], lon_in.at[i, 0], halo_ss.at[i, 2], halo_rs.at[i, 2], {"tile": east}),
            remote(lon_out.at[i, 1], lon_in.at[i, 1], halo_ss.at[i, 3], halo_rs.at[i, 3], {"tile": west}),
        ]

    def stage_lon(x, i):
        for t in range(TR):
            for l in range(LV):
                lon_out[i, 0, t * LV + l : t * LV + l + 1, :] = x[t, l + 1, LON - 1 : LON, :]
                lon_out[i, 1, t * LV + l : t * LV + l + 1, :] = x[t, l + 1, 0:1, :]

    def finish_halo(x, i, copies):
        for copy in copies:
            copy.wait_recv()

        @pl.when(lev == NLEV - 1)
        def _():
            x[:, LV + 1] = jnp.zeros((TR, LON, LAT), F32)

        @pl.when(tile == NTILE - 1)
        def _():
            lon_in[i, 1] = jnp.zeros((24, LAT), F32)

    pl.semaphore_wait(barrier, NTILE - 1 + NLEV - 1)

    for copy in loads:
        copy.wait()
    halo = [lev_copies(x0, 0)]
    k_copy = remote(k.at[LV], k.at[0], halo_ss.at[0, 4], halo_rs.at[0, 4], {"lev": above})
    for copy in halo[0] + [k_copy]:
        copy.start()
    stage_lon(x0, 0)
    for l in range(LV):
        lon_out[0, 0, 18 + l : 19 + l, :] = u[l, LON - 1 : LON, :]
    lons = [lon_copies(0)]
    for copy in lons[0]:
        copy.start()

    target = fields[13:14, :].astype(jnp.int32)
    match = (lax.broadcasted_iota(jnp.int32, (NTILE, SND), 0) == target).astype(F32)
    earlier = (
        lax.broadcasted_iota(jnp.int32, (SND, SND), 0) < lax.broadcasted_iota(jnp.int32, (SND, SND), 1)
    ).astype(F32).astype(BF16)
    before = jnp.dot(match.astype(BF16), earlier, preferred_element_type=F32)
    rank = jnp.sum(before * match, axis=0, keepdims=True).astype(jnp.int32)
    slot = target * CAP + rank
    for i in range(NLEV):
        hot[i * CHUNK : (i + 1) * CHUNK, :] = (
            (lax.broadcasted_iota(jnp.int32, (CHUNK, SND), 0) + i * CHUNK == slot).astype(F32).astype(BF16)
        )
    data = jnp.concatenate([p.astype(F32) for p in parts_of(fields[...], 3)], axis=0).astype(BF16)

    def pack(i, carry):
        rows = pl.ds(pl.multiple_of(i * CHUNK, CHUNK), CHUNK)
        got = lax.dot_general(data, hot[rows, :], NT, preferred_element_type=F32)
        got = got[0:16] + got[16:32] + got[32:48]
        for h in range(2):
            a, b = got[0:8, h * 128 : h * 128 + 128], got[8:16, h * 128 : h * 128 + 128]
            ids_out[i * 4 + h * 2] = jnp.where(row8, a, pltpu.roll(b, CAP, 1))
            ids_out[i * 4 + h * 2 + 1] = jnp.where(row8, pltpu.roll(a, CAP, 1), b)
        return carry

    lax.fori_loop(0, NLEV, pack, 0)
    ids_in[tile] = ids_out[tile]

    def ids_copy(d):
        peer = lax.rem(tile + d, NTILE)
        return remote(ids_out.at[peer], ids_in.at[tile], ids_ss.at[d], ids_rs.at[d], {"tile": peer})

    def ids_wait(d, carry):
        source = lax.rem(tile + NTILE - d, NTILE)
        remote(
            ids_out.at[source], ids_in.at[source], ids_ss.at[d], ids_rs.at[d], {"tile": source}
        ).wait_recv()
        return carry

    def start(make):
        def step(d, carry):
            make(d).start()
            return carry
        return step

    def sent(make):
        def step(d, carry):
            make(d).wait_send()
            return carry
        return step

    lax.fori_loop(1, NTILE, start(ids_copy), 0)

    last_row = lax.broadcasted_iota(jnp.int32, (LON, LAT), 0) == LON - 1
    first_row = lax.broadcasted_iota(jnp.int32, (LON, LAT), 0) == 0
    open_face = lax.broadcasted_iota(jnp.int32, (LON, LAT), 1) < LAT - 1

    def sweep(x, i, adjoint, levels, put):
        for l in levels:
            ul, kl, kb = u[l], k[l + 1], k[l]
            uw = jnp.where(first_row, lon_in[0, 0, 18 + l : 19 + l, :], pltpu.roll(ul, 1, 0))
            vl = jnp.where(open_face, v[l], 0.0)
            a, bw = jnp.maximum(ul, 0.0), jnp.minimum(uw, 0.0)
            p, q = jnp.maximum(vl, 0.0), jnp.minimum(vl, 0.0)
            if adjoint:
                qs = pltpu.roll(q, 1, 1)
            else:
                b, aw = jnp.minimum(ul, 0.0), jnp.maximum(uw, 0.0)
            for t in range(TR):
                r = t * LV + l
                c = x[t, l + 1]
                ce = jnp.where(last_row, lon_in[i, 1, r : r + 1, :], pltpu.roll(c, LON - 1, 0))
                cw = jnp.where(first_row, lon_in[i, 0, r : r + 1, :], pltpu.roll(c, 1, 0))
                cn = pltpu.roll(c, LAT - 1, 1)
                vert = kl * (x[t, l + 2] - c) - kb * (c - x[t, l])
                if adjoint:
                    cs = pltpu.roll(c, 1, 1)
                    y = c + (a * (ce - c) + bw * (c - cw)) + (p * (cn - c) + qs * (c - cs)) + vert
                else:
                    fn = p * c + q * cn
                    y = c - (a * c + b * ce) + (aw * cw + bw * c) - fn + pltpu.roll(fn, 1, 1) + vert
                put(t, l, y)

    def put_in(x):
        def put(t, l, y):
            x[t, l + 1] = y
        return put

    def two_sweeps(first, second, i, adjoint, put):
        sweep(first, i, adjoint, (0, LV - 1), put_in(second))
        halo.append(lev_copies(second, i + 1))
        for copy in halo[-1]:
            copy.start()
        sweep(first, i, adjoint, range(1, LV - 1), put_in(second))
        stage_lon(second, i + 1)
        lons.append(lon_copies(i + 1))
        for copy in lons[-1]:
            copy.start()

    finish_halo(x0, 0, halo[0] + lons[0] + [k_copy])

    @pl.when(lev == 0)
    def _():
        k[0] = jnp.zeros((LON, LAT), F32)

    @pl.when(tile == 0)
    def _():
        lon_in[0, 0, 18:24] = jnp.zeros((6, LAT), F32)

    two_sweeps(x0, x1, 0, False, None)

    lax.fori_loop(1, NTILE, ids_wait, 0)

    def unpack(c, carry):
        left, right = [], []
        for h in range(2):
            a, b = ids_in[c * 4 + h * 2], ids_in[c * 4 + h * 2 + 1]
            left.append(jnp.where(row8, a, pltpu.roll(b, CAP, 1)))
            right.append(jnp.where(row8, pltpu.roll(a, CAP, 1), b))
        ga, gb = jnp.concatenate(left, axis=1), jnp.concatenate(right, axis=1)
        fb[c] = gb
        ga = ga.astype(jnp.int32)
        kind = gb[0:1, :].astype(jnp.int32)
        weights = jnp.zeros((LV, CHUNK), F32)
        for j in range(8):
            weights = weights + jnp.where(kind == j, kern[:, j : j + 1], 0.0)
        kw[c, 0:LV, :] = weights
        for j in range(FOOT):
            cols = slice(j * CHUNK, (j + 1) * CHUNK)
            lat = (lax.broadcasted_iota(jnp.int32, (LAT, CHUNK), 0) == ga[j : j + 1, :]).astype(F32).astype(BF16)
            lathot[c, 0:LAT, cols] = lat
            lathot[c, LAT : 2 * LAT, cols] = lat
            lonhot[c, :, cols] = (
                lax.broadcasted_iota(jnp.int32, (LON, CHUNK), 0) == ga[4 + j : 5 + j, :]
            ).astype(F32)
        return carry

    lax.fori_loop(0, NLEV, unpack, 0)

    finish_halo(x1, 1, halo[1] + lons[1])

    def put_evolved(t, l, y):
        r = (t * LV + l) * LON
        high, low = parts_of(y, 2)
        e[r : r + LON, 0:LAT] = high
        e[r : r + LON, LAT : 2 * LAT] = low

    sweep(x1, 1, False, range(LV), put_evolved)

    def part_copy(d):
        peer = lax.rem(lev + d, NLEV)
        return remote(part_out.at[peer], part_in.at[lev], part_ss.at[d], part_rs.at[d], {"lev": peer})

    def gather(c, carry):
        picked[...] = jnp.dot(e[...], lathot[c], preferred_element_type=F32)
        mask = lonhot[c]
        for t in range(TR):
            acc = jnp.zeros((LON, CHUNK), F32)
            for l in range(LV):
                r = (t * LV + l) * LON
                block = picked[r : r + LON, :] * mask
                block = (block[:, 0:CHUNK] + block[:, CHUNK : 2 * CHUNK]) + (
                    block[:, 2 * CHUNK : 3 * CHUNK] + block[:, 3 * CHUNK :]
                )
                acc = acc + block * kw[c, l : l + 1, :]
            row = jnp.sum(acc, axis=0, keepdims=True)
            part_out[c, t : t + 1, :] = row[:, 0:128]
            part_out[c, 3 + t : 4 + t, :] = row[:, 128:256]
        return carry

    def gather_at(d, carry):
        gather(lax.rem(lev + d, NLEV), 0)
        part_copy(d).start()
        return carry

    lax.fori_loop(1, NLEV, gather_at, 0)
    gather(lev, 0)
    part_in[lev] = part_out[lev]

    def part_wait(d, carry):
        source = lax.rem(lev + NLEV - d, NLEV)
        remote(
            part_out.at[source], part_in.at[source], part_ss.at[d], part_rs.at[d], {"lev": source}
        ).wait_recv()
        return carry

    lax.fori_loop(1, NLEV, part_wait, 0)
    model = part_in[0]
    for z in range(1, NLEV):
        model = model + part_in[z]
    own = fb[lev]
    seen = jnp.concatenate([own[1:4, 0:128], own[1:4, 128:256]], axis=0)
    res[lev, 0:6] = model[0:6] * (1.0 / FOOT) - seen

    def res_copy(d):
        peer = lax.rem(lev + d, NLEV)
        return remote(res.at[lev], res.at[lev], res_ss.at[d], res_rs.at[d], {"lev": peer})

    def res_wait(d):
        source = lax.rem(lev + NLEV - d, NLEV)
        remote(res.at[source], res.at[source], res_ss.at[d], res_rs.at[d], {"lev": source}).wait_recv()

    lax.fori_loop(1, NLEV, start(res_copy), 0)

    def scatter(c):
        mask = lonhot[c]
        for t in range(TR):
            row = jnp.concatenate([res[c, t : t + 1, :], res[c, 3 + t : 4 + t, :]], axis=1)
            row = row * fb[c, 4:5, :] * (1.0 / FOOT)
            for l in range(LV):
                r = (t * LV + l) * LON
                high, low = parts_of(row * kw[c, l : l + 1, :], 2)
                for h, piece in enumerate((high, low)):
                    piece = piece.astype(F32)
                    for j in range(FOOT):
                        cols = slice(j * CHUNK, (j + 1) * CHUNK)
                        terms[h * ROWS + r : h * ROWS + r + LON, cols] = (mask[:, cols] * piece).astype(BF16)
        return lax.dot_general(terms[...], lathot[c, 0:LAT, :], NT, preferred_element_type=F32)

    total[...] = scatter(lev)

    def scatter_at(d, carry):
        res_wait(d)
        total[...] += scatter(lax.rem(lev + NLEV - d, NLEV))
        return carry

    lax.fori_loop(1, NLEV, scatter_at, 0)

    def ret_copy(d):
        peer = lax.rem(tile + d, NTILE)
        return remote(res.at[peer // 4], ret_in.at[tile], ret_ss.at[d], ret_rs.at[d], {"tile": peer})

    def ret_wait(d, carry):
        source = lax.rem(tile + NTILE - d, NTILE)
        remote(
            res.at[source // 4], ret_in.at[source], ret_ss.at[d], ret_rs.at[d], {"tile": source}
        ).wait_recv()
        return carry

    lax.fori_loop(1, NTILE, start(ret_copy), 0)
    ret_in[tile] = res[tile // 4]

    for t in range(TR):
        for l in range(LV):
            r = (t * LV + l) * LON
            x2[t, l + 1] = total[r : r + LON, :] + total[ROWS + r : ROWS + r + LON, :]
    halo.append(lev_copies(x2, 2))
    for copy in halo[2]:
        copy.start()
    stage_lon(x2, 2)
    lons.append(lon_copies(2))
    for copy in lons[2]:
        copy.start()

    lax.fori_loop(1, NTILE, ret_wait, 0)
    pair_odd, odd = lax.rem(tile // 2, 2) == 1, lax.rem(tile, 2) == 1
    for i in range(NTILE // 2):
        halves = []
        for h in range(2):
            got = ret_in[2 * i + h]
            got = jnp.where(pair_odd, pltpu.roll(got, 5, 0), got)
            moved = pltpu.roll(got, CAP, 1)
            halves.append(jnp.where(odd, got, moved) if h else jnp.where(odd, moved, got))
        both = jnp.where(row8, halves[0], halves[1])
        keep = lax.broadcasted_iota(jnp.int32, (8, 128), 0) < TR
        for j, piece in enumerate(parts_of(jnp.where(keep, both, 0.0), 3)):
            spread[j, :, i * 128 : (i + 1) * 128] = piece.astype(F32)
    back = jnp.concatenate([spread[0], spread[1], spread[2], jnp.zeros((8, SLOTS), F32)], axis=0).astype(BF16)
    back = jnp.dot(back, hot[...], preferred_element_type=F32)
    residual[...] = (back[0:8] + back[8:16] + back[16:24])[0:TR]

    finish_halo(x2, 2, halo[2] + lons[2])
    two_sweeps(x2, x3, 2, True, None)
    finish_halo(x3, 3, halo[3] + lons[3])

    def put_gradient(t, l, y):
        gradient[t, l] = y

    sweep(x3, 3, True, range(LV), put_gradient)

    for copies in halo + lons + [[k_copy]]:
        for copy in copies:
            copy.wait_send()
    lax.fori_loop(1, NTILE, sent(ids_copy), 0)
    lax.fori_loop(1, NLEV, sent(part_copy), 0)
    lax.fori_loop(1, NLEV, sent(res_copy), 0)
    lax.fori_loop(1, NTILE, sent(ret_copy), 0)


def body(conc, u_wind, v_wind, mixing, kernels, observed, obs_weight, column_tile, footprint, kernel_index):
    feet = footprint.T
    lon = (feet // LAT).astype(F32)
    lat = (feet % LAT).astype(F32)
    fields = jnp.concatenate(
        [
            lat,
            lon,
            kernel_index[None].astype(F32),
            observed,
            obs_weight[None],
            column_tile.T.astype(F32),
            jnp.zeros((2, SND), F32),
        ],
        axis=0,
    )
    dma = pltpu.SemaphoreType.DMA
    anywhere, vmem = pl.BlockSpec(memory_space=pl.ANY), pl.BlockSpec(memory_space=pltpu.VMEM)
    ext = pltpu.VMEM((TR, LV + 2, LON, LAT), F32)
    return pl.pallas_call(
        kernel,
        out_shape=(
            jax.ShapeDtypeStruct((TR, SND), F32),
            jax.ShapeDtypeStruct((TR, LV, LON, LAT), F32),
        ),
        in_specs=[anywhere] * 4 + [vmem] * 2,
        out_specs=(vmem, vmem),
        scratch_shapes=[
            ext, ext, ext, ext,
            pltpu.VMEM((LV, LON, LAT), F32),
            pltpu.VMEM((LV, LON, LAT), F32),
            pltpu.VMEM((LV + 1, LON, LAT), F32),
            pltpu.VMEM((4, 2, 24, LAT), F32),
            pltpu.VMEM((4, 2, 24, LAT), F32),
            pltpu.VMEM((NTILE, 8, 128), F32),
            pltpu.VMEM((NTILE, 8, 128), F32),
            pltpu.VMEM((SLOTS, SND), BF16),
            pltpu.VMEM((NLEV, 8, CHUNK), F32),
            pltpu.VMEM((NLEV, 8, CHUNK), F32),
            pltpu.VMEM((NLEV, 8, CHUNK), F32),
            pltpu.VMEM((NLEV, 2 * LAT, LOOK), BF16),
            pltpu.VMEM((NLEV, LON, LOOK), F32),
            pltpu.VMEM((3, 8, SLOTS), F32),
            pltpu.VMEM((ROWS, 2 * LAT), BF16),
            pltpu.VMEM((ROWS, LOOK), F32),
            pltpu.VMEM((NLEV, 8, 128), F32),
            pltpu.VMEM((NLEV, 8, 128), F32),
            pltpu.VMEM((NLEV, 8, 128), F32),
            pltpu.VMEM((NTILE, 8, 128), F32),
            pltpu.VMEM((2 * ROWS, LOOK), BF16),
            pltpu.VMEM((2 * ROWS, LAT), F32),
            dma((4,)),
            dma((4, 5)), dma((4, 5)),
            dma((NTILE,)), dma((NTILE,)),
            dma((NLEV,)), dma((NLEV,)),
            dma((NLEV,)), dma((NLEV,)),
            dma((NTILE,)), dma((NTILE,)),
        ],
        compiler_params=pltpu.CompilerParams(
            collective_id=0, has_side_effects=True, vmem_limit_bytes=56 * 1024 * 1024
        ),
    )(conc, u_wind, v_wind, mixing, kernels.T, fields)


def solution(mesh):
    placed = (
        P(None, "lev", "tile", None),
        P("lev", "tile", None),
        P("lev", "tile", None),
        P("lev", "tile", None),
        P(None, "lev"),
        P(None, "tile"),
        P("tile"),
        P("tile", None),
        P("tile", None),
        P("tile"),
    )
    return jax.shard_map(
        body,
        mesh=mesh,
        in_specs=placed,
        out_specs=(P(None, "tile"), P(None, "lev", "tile", None)),
        check_vma=False,
    )
```

time: 373 us -> 73.6 us (0.20)
  local copies, waits for them, and re-layouts: 121 us -> 6.78 us
  other arithmetic: 105 us -> 1.42 us
  starting transfers between devices: 80.3 us -> 0 us
  Pallas kernels: 0 us -> 64.4 us
  blocking collectives: 38.2 us -> 0 us
  waiting for transfers between devices: 19.3 us -> 0 us
  matrix products: 4.55 us -> 0 us
    scatter-add x1 -> x0, other arithmetic: 69.1 us -> none  [body(): summed = jnp.zeros((tracer_count, kind_count * col_count), jnp.float32).a...]
    pallas_call x0 -> x1, Pallas kernels: none -> 64.4 us  [body(): pl.pallas_call(kernel, out_shape=(jax.ShapeDtypeStruct((TR, SND), F32), j...]
    ppermute x18 -> x0, starting transfers between devices: 55.8 us -> none  [the longest x8 30.5 us: padded_2(): before = lax.ppermute(last, axis, up)]
    reshape x4 -> x0, local copies, waits for them, and re-layouts: 53.6 us -> none  [the longest x1 27 us: body(): summed.reshape(tracer_count, kind_count, col_count)]
    gather x2 -> x0, local copies, waits for them, and re-layouts: 47.4 us -> none  [the longest x1 43.3 us: body(): jnp.take(profile_flat, flat_index.reshape(-1), axis=1)]
    psum x1 -> x0, blocking collectives: 27.5 us -> none  [body(): model_in = lax.psum(partial_value, 'lev') / foot_count]
    all_to_all x2 -> x0, starting transfers between devices: 24.6 us -> none  [the longest x1 15.8 us: body(): lax.all_to_all(model_in, 'tile', split_axis=1, concat_axis=1, tiled=True)]
    ppermute x18 -> x0, waiting for transfers between devices: 12.4 us -> none  [the longest x8 6.53 us: padded_2(): after = lax.ppermute(leading, axis, down)]
  transfers between devices with their start and end apart: 20 -> 0, of which waited for: 9 -> 0; matrix products, arithmetic and copies ran while one was open for 9% -> 0% of each run, Pallas kernels for 0% -> 0%
where the time goes in v1:
time: 73.6 us; the launch traced here: 73.2 us
  Pallas kernels  64.4 us (88%)
  local copies, waits for them, and re-layouts  6.78 us (9%)
  other arithmetic  1.42 us (2%)
    pallas_call x1, Pallas kernels, body(): pl.pallas_call(kernel, out_shape=(jax.ShapeDtypeStruct((TR, SND), F32), j...  64.4 us
    unnamed x9, local copies, waits for them, and re-layouts  5.5 us

profile of v1, /device:TPU:1, one launch (start us, length us, event | category | flops | bytes accessed | tf_op | source)
XLA Modules:
  0.0 73.2 jit_solution(13413991000685625807)
XLA Ops:
  0.6 0.0 copy-start
  0.6 1.4 %copy.12 = f32[8,6]{0,1:T(8,128)} copy(f32[8,6]{1,0:T(8,128)} %param.14) | data formatting | bytes 384 | tf_op args[4]
  2.0 0.7 convert_bitcast_fusion
  2.7 0.7 convert_element_type.28
  3.4 0.0 copy-done
  3.4 0.0 copy-start.1
  3.4 0.0 copy-start.2
  3.4 0.7 copy-done.1
  4.1 0.0 copy-done.2
  4.1 1.3 %concatenate.3.fields = f32[16,1024]{1,0:T(8,128)} concatenate(f32[4,1024]{1,0:T(4,128)S(1)} %get-tuple-element.3, f32[4,1024]{1,0:T(4,128)S(1)} %get-tuple-element.2, f32[1,1024]{1,0:T(1,128)S(1)} %bitcast.26, f32[3,1024]{1,0:T(4,128)S(1)} %copy-done.1, f32[1,1024]{1,0:T(1,128)S(1)} %bitcast.27, f32[1,1024]{1,0:T(1,128)S(1)} %convert_bitcast_fusion, f32[2,1024]{1,0:T(2,128)S(1)} %broadcast_in_dim.8), dimensions={0} | concatenate | bytes 131072 | tf_op jit(solution)/shard_map/concatenate | solution.py:411
  5.4 64.4 %shard_map.113 = (f32[3,1024]{1,0:T(4,128)}, f32[3,6,32,384]{3,2,1,0:T(8,128)}) custom-call(f32[3,6,32,384]{3,2,1,0:T(8,128)} %conc.1, f32[6,32,384]{2,1,0:T(8,128)} %u_in.1, f32[6,32,384]{2,1,0:T(8,128)} %v_in.1, f32[6,32,384]{2,1,0:T(8,128)} %k_in.1, f32[6,8]{1,0:T(8,128)} %bitcast.25, f32[16,1024]{1,0:T(8,128)} %concatenate.3.fields), custom_call_target="tpu_custom_call" | custom-call | tf_op jit(solution)/shard_map/pallas_call | solution.py:426
  69.8 1.3 %copy.15 = f32[3,1024]{1,0:T(4,128)} copy(f32[3,1024]{1,0:T(4,128)} %get-tuple-element.6) | data formatting | bytes 24576
  71.1 2.1 %copy.16 = f32[3,6,32,384]{3,2,1,0:T(8,128)} copy(f32[3,6,32,384]{3,2,1,0:T(8,128)} %get-tuple-element.7) | data formatting | bytes 1769472
  (2 shorter events, 0.0 us)
Async XLA Ops:
  0.6 2.8 %copy-start = (s32[1024,4]{0,1:T(4,128)S(1)}, s32[1024,4]{0,1:T(4,128)}, u32[]{:S(2)}) copy-start(s32[1024,4]{0,1:T(4,128)} %param.18) | copy-start | bytes 49156
  3.4 0.7 copy-start.1
  3.4 0.7 copy-start.2

commit v2 on v0

v2 whole, which is shorter than its diff:
```python
import jax
import jax.numpy as jnp
from jax import lax
from jax.experimental import pallas as pl
from jax.experimental.pallas import tpu as pltpu
from jax.sharding import PartitionSpec as P

MESH = pl.DeviceIdType.MESH
F32, BF16, I32 = jnp.float32, jnp.bfloat16, jnp.int32
NT = (((1,), (1,)), ((), ()))
TR, LV, LON, LAT, KIND = 3, 6, 32, 384, 8
EXT = LV + 4
ROWS = TR * KIND * LON
PER = KIND * LON
NTILE, NLEV, CAP, SND, FOOT = 32, 8, 64, 1024, 4
SLOTS = NTILE * CAP
CHUNK = SLOTS // NLEV
LOOK = FOOT * CHUNK


def parts_of(x, count):
    pieces = []
    for _ in range(count):
        piece = x.astype(BF16)
        pieces.append(piece)
        x = x - piece.astype(F32)
    return pieces


def onehot(rows, index, base=0):
    shape = (rows, index.shape[1])
    return (lax.broadcasted_iota(I32, shape, 0) + base == index).astype(F32)


def loop(low, high, body):
    def step(i, carry):
        body(i)
        return carry

    lax.fori_loop(low, high, step, 0)


def kernel(
    conc, u_in, v_in, k_in, kern, observed, weight, column, feet, kinds,
    residual, gradient,
    x0, x1, x2, x3, u, v, k, lon_out, lon_in, kern_all, kern_wide, fields,
    ids_out, ids_in, hot, fb, kindhot, lathot, lonhot, lonbits, spread,
    e, picked, part_out, part_in, res, ret_in, terms, total,
    local_sem, lev_ss, lev_rs, lon_ss, lon_rs, ids_ss, ids_rs, part_ss, part_rs, ret_ss, ret_rs,
):
    tile, lev = lax.axis_index("tile"), lax.axis_index("lev")
    east, west = lax.rem(tile + 1, NTILE), lax.rem(tile + NTILE - 1, NTILE)
    above, below = lax.rem(lev + 1, NLEV), lax.rem(lev + NLEV - 1, NLEV)

    def remote(src, dst, ss, rs, target):
        return pltpu.make_async_remote_copy(
            src_ref=src, dst_ref=dst, send_sem=ss, recv_sem=rs, device_id=target, device_id_type=MESH
        )

    barrier = pltpu.get_barrier_semaphore()

    def greet(target):
        pl.semaphore_signal(barrier, inc=1, device_id=target, device_id_type=MESH)

    loop(1, NLEV, lambda d: greet({"lev": lax.rem(lev + d, NLEV)}))
    loop(1, NTILE, lambda d: greet({"tile": lax.rem(tile + d, NTILE)}))
    own = pl.ds(2, LV)
    loads = [
        pltpu.make_async_copy(conc, x0.at[:, own], local_sem.at[0]),
        pltpu.make_async_copy(u_in, u.at[pl.ds(1, LV)], local_sem.at[1]),
        pltpu.make_async_copy(v_in, v.at[pl.ds(1, LV)], local_sem.at[2]),
        pltpu.make_async_copy(k_in, k.at[own], local_sem.at[3]),
    ]
    for copy in loads:
        copy.start()

    half = lax.broadcasted_iota(I32, (8, 128), 1) < CAP

    foot = feet[...]
    foot_lon = lax.shift_right_logical(lax.shift_right_logical(foot, 7) * 171, 9)
    fields[0:4, :] = (foot - foot_lon * LAT).astype(F32)
    fields[4:8, :] = foot_lon.astype(F32)
    fields[8:9, :] = kinds[...].astype(F32)
    fields[9:12, :] = observed[...]
    fields[12:13, :] = weight[...]
    fields[13:16, :] = jnp.zeros((3, SND), F32)
    target = column[...]
    match = onehot(NTILE, target)
    earlier = (
        lax.broadcasted_iota(I32, (SND, SND), 0) < lax.broadcasted_iota(I32, (SND, SND), 1)
    ).astype(F32).astype(BF16)
    before = jnp.dot(match.astype(BF16), earlier, preferred_element_type=F32)
    slot = target * CAP + jnp.sum(before * match, axis=0, keepdims=True).astype(I32)
    data = jnp.concatenate([p.astype(F32) for p in parts_of(fields[...], 3)], axis=0).astype(BF16)

    def pack(i):
        rows = pl.ds(pl.multiple_of(i * CHUNK, CHUNK), CHUNK)
        hot[rows, :] = onehot(CHUNK, slot, i * CHUNK).astype(BF16)
        got = lax.dot_general(data, hot[rows, :], NT, preferred_element_type=F32)
        got = got[0:16] + got[16:32] + got[32:48]
        for h in range(2):
            a, b = got[0:8, h * 128 : h * 128 + 128], got[8:16, h * 128 : h * 128 + 128]
            ids_out[i * 4 + h * 2] = jnp.where(half, a, pltpu.roll(b, CAP, 1))
            ids_out[i * 4 + h * 2 + 1] = jnp.where(half, pltpu.roll(a, CAP, 1), b)

    loop(0, NLEV, pack)
    ids_in[tile] = ids_out[tile]
    kern_all[0, :, 0:LV] = kern[...]

    blank = jnp.zeros((TR, LON, LAT), F32)
    x0[:, 1], x0[:, 8] = blank, blank
    x1[:, 0], x1[:, 9] = blank, blank

    def lon_copies(i):
        return [
            remote(lon_out.at[i, 0], lon_in.at[i, 0], lon_ss.at[i, 0], lon_rs.at[i, 0], {"tile": east}),
            remote(lon_out.at[i, 1], lon_in.at[i, 1], lon_ss.at[i, 1], lon_rs.at[i, 1], {"tile": west}),
        ]

    def stage_lon(x, i, low, high):
        def one(n):
            for t in range(TR):
                lon_out[i, 0, t * 8 + n - 1] = x[t, n, LON - 1]
                lon_out[i, 1, t * 8 + n - 1] = x[t, n, 0]
            if i < 2:
                lon_out[i, 0, 23 + n] = u[n - 1, LON - 1]

        loop(low, high, one)

    def finish_lon(i):
        for copy in lons[i]:
            copy.wait_recv()

        @pl.when(tile == NTILE - 1)
        def _():
            lon_in[i, 1] = jnp.zeros((32, LAT), F32)

        if i < 2:

            @pl.when(tile == 0)
            def _():
                lon_in[i, 0, 24:32] = jnp.zeros((8, LAT), F32)

    for copy in loads:
        copy.wait()
    stage_lon(x0, 0, 2, 8)

    lev_moves = [
        (k.at[pl.ds(LV, 2)], k.at[pl.ds(0, 2)], above),
        (kern_all.at[0], kern_all.at[1], above),
        (kern_all.at[0], kern_all.at[2], below),
        (u.at[LV], u.at[0], above),
        (u.at[1], u.at[LV + 1], below),
        (v.at[LV], v.at[0], above),
        (v.at[1], v.at[LV + 1], below),
        (k.at[2], k.at[LV + 2], below),
    ]
    lev_copies = [
        remote(src, dst, lev_ss.at[n], lev_rs.at[n], {"lev": to}) for n, (src, dst, to) in enumerate(lev_moves)
    ]
    lons = [lon_copies(0)]

    def ids_copy(d):
        peer = lax.rem(tile + d, NTILE)
        return remote(ids_out.at[peer], ids_in.at[tile], ids_ss.at[d], ids_rs.at[d], {"tile": peer})

    def ids_wait(d):
        source = lax.rem(tile + NTILE - d, NTILE)
        remote(ids_out.at[source], ids_in.at[source], ids_ss.at[d], ids_rs.at[d], {"tile": source}).wait_recv()

    pl.semaphore_wait(barrier, NTILE - 1 + NLEV - 1)
    for copy in lons[0] + lev_copies:
        copy.start()
    loop(1, NTILE, lambda d: ids_copy(d).start())

    last_row = lax.broadcasted_iota(I32, (LON, LAT), 0) == LON - 1
    first_row = lax.broadcasted_iota(I32, (LON, LAT), 0) == 0
    open_face = lax.broadcasted_iota(I32, (LON, LAT), 1) < LAT - 1

    def sweep(x, i, adjoint, low, high, put):
        def one(n):
            ul, kl, kb = u[n - 1], k[n], k[n - 1]
            uw = jnp.where(first_row, lon_in[min(i, 1), 0, pl.ds(23 + n, 1), :], pltpu.roll(ul, 1, 0))
            vl = jnp.where(open_face, v[n - 1], 0.0)
            a, bw = jnp.maximum(ul, 0.0), jnp.minimum(uw, 0.0)
            p, q = jnp.maximum(vl, 0.0), jnp.minimum(vl, 0.0)
            if adjoint:
                qs = pltpu.roll(q, 1, 1)
            else:
                b, aw = jnp.minimum(ul, 0.0), jnp.maximum(uw, 0.0)
            for t in range(TR):
                row = pl.ds(t * 8 + n - 1, 1)
                c = x[t, n]
                ce = jnp.where(last_row, lon_in[i, 1, row, :], pltpu.roll(c, LON - 1, 0))
                cw = jnp.where(first_row, lon_in[i, 0, row, :], pltpu.roll(c, 1, 0))
                cn = pltpu.roll(c, LAT - 1, 1)
                vert = kl * (x[t, n + 1] - c) - kb * (c - x[t, n - 1])
                if adjoint:
                    cs = pltpu.roll(c, 1, 1)
                    y = c + (a * (ce - c) + bw * (c - cw)) + (p * (cn - c) + qs * (c - cs)) + vert
                else:
                    fn = p * c + q * cn
                    y = c - (a * c + b * ce) + (aw * cw + bw * c) - fn + pltpu.roll(fn, 1, 1) + vert
                put(t, n, y)

        loop(low, high, one)

    def put_in(x):
        def put(t, n, y):
            x[t, n] = y

        return put

    lev_copies[0].wait_recv()

    @pl.when(lev == 0)
    def _():
        k[0:2] = jnp.zeros((2, LON, LAT), F32)

    finish_lon(0)
    sweep(x0, 0, False, 2, 8, put_in(x1))
    for t in range(TR):
        x1[t, 1] = k[1] * x0[t, 2]
        x1[t, 8] = k[7] * x0[t, 7]

    @pl.when(lev == NLEV - 1)
    def _():
        x1[:, 8] = blank

    for copy in lev_copies[1:]:
        copy.wait_recv()
    stage_lon(x1, 1, 1, 9)
    lons.append(lon_copies(1))
    for copy in lons[1]:
        copy.start()

    @pl.when(lev == 0)
    def _():
        kern_all[1] = jnp.zeros((KIND, 128), F32)

    @pl.when(lev == NLEV - 1)
    def _():
        kern_all[2] = jnp.zeros((KIND, 128), F32)

    for n in range(EXT):
        which, col = (1, 4 + n) if n < 2 else (0, n - 2) if n < 8 else (2, n - 8)
        kern_wide[n] = jnp.broadcast_to(kern_all[which, :, col : col + 1], (KIND, 128))

    loop(1, NTILE, ids_wait)

    def unpack(c):
        left, right = [], []
        for h in range(2):
            a, b = ids_in[c * 4 + h * 2], ids_in[c * 4 + h * 2 + 1]
            left.append(jnp.where(half, a, pltpu.roll(b, CAP, 1)))
            right.append(jnp.where(half, pltpu.roll(a, CAP, 1), b))
        ga, gb = jnp.concatenate(left, axis=1), jnp.concatenate(right, axis=1)
        fb[c] = gb
        ga = ga.astype(I32)
        kindhot[c] = onehot(KIND, gb[0:1, :].astype(I32))
        for j in range(FOOT):
            cols = slice(j * CHUNK, (j + 1) * CHUNK)
            lat = onehot(LAT, ga[j : j + 1, :]).astype(BF16)
            lathot[c, 0:LAT, cols] = lat
            lathot[c, LAT : 2 * LAT, cols] = lat
            lon = onehot(LON, ga[4 + j : 5 + j, :])
            lonhot[c, :, cols] = lon
            lonbits[c, :, cols] = lon.astype(BF16)

    loop(0, NLEV, unpack)

    finish_lon(1)
    sweep(x1, 1, False, 1, 9, put_in(x2))
    for t in range(TR):
        x2[t, 0] = k[0] * x1[t, 1]
        x2[t, 9] = k[8] * x1[t, 8]

    def profile(i):
        t, h = i // 2, lax.rem(i, 2)
        rows = pl.ds(pl.multiple_of(h * 16, 16), 16)
        for w in range(LAT // 128):
            cols = slice(w * 128, (w + 1) * 128)
            planes = [x2[t, n, rows, cols] for n in range(EXT)]
            for j in range(KIND):
                acc = planes[0] * kern_wide[0, j : j + 1, :]
                for n in range(1, EXT):
                    acc = acc + planes[n] * kern_wide[n, j : j + 1, :]
                high, low = parts_of(acc, 2)
                to = pl.ds(pl.multiple_of(t * PER + j * LON + h * 16, 16), 16)
                e[to, cols] = high
                e[to, LAT + w * 128 : LAT + (w + 1) * 128] = low

    loop(0, 2 * TR, profile)

    def part_copy(c, d):
        peer = lax.rem(lev + d, NLEV)
        return remote(part_out.at[c], part_in.at[lev, c], part_ss.at[c, d], part_rs.at[c, d], {"lev": peer})

    def part_wait(c, d):
        source = lax.rem(lev + NLEV - d, NLEV)
        remote(
            part_out.at[c], part_in.at[source, c], part_ss.at[c, d], part_rs.at[c, d], {"lev": source}
        ).wait_recv()

    def gather(c):
        picked[...] = jnp.dot(e[...], lathot[c], preferred_element_type=F32)
        mask = lonhot[c]
        for t in range(TR):
            acc = jnp.zeros((LON, CHUNK), F32)
            for j in range(KIND):
                r = t * PER + j * LON
                block = picked[r : r + LON, :] * mask
                block = (block[:, 0:CHUNK] + block[:, CHUNK : 2 * CHUNK]) + (
                    block[:, 2 * CHUNK : 3 * CHUNK] + block[:, 3 * CHUNK :]
                )
                acc = acc + block * kindhot[c, j : j + 1, :]
            row = jnp.sum(acc, axis=0, keepdims=True)
            part_out[c, t : t + 1, :] = row[:, 0:128]
            part_out[c, 3 + t : 4 + t, :] = row[:, 128:256]
        part_in[lev, c] = part_out[c]
        for d in range(1, NLEV):
            part_copy(c, d).start()

    loop(0, NLEV, gather)

    def ret_copy(peer):
        d = lax.rem(peer + NTILE - tile, NTILE)
        return remote(res.at[peer // 4], ret_in.at[tile], ret_ss.at[d], ret_rs.at[d], {"tile": peer})

    def ret_wait(d):
        source = lax.rem(tile + NTILE - d, NTILE)
        remote(res.at[source // 4], ret_in.at[source], ret_ss.at[d], ret_rs.at[d], {"tile": source}).wait_recv()

    total[...] = jnp.zeros((ROWS, LAT), F32)

    def scatter(c):
        for d in range(1, NLEV):
            part_wait(c, d)
        model = part_in[0, c]
        for z in range(1, NLEV):
            model = model + part_in[z, c]
        seen = jnp.concatenate([fb[c, 1:4, 0:128], fb[c, 1:4, 128:256]], axis=0)
        res[c, 0:6] = model[0:6] * (1.0 / FOOT) - seen
        for n in range(4):
            peer = c * 4 + n

            @pl.when(peer != tile)
            def _():
                ret_copy(peer).start()

        mask = lonbits[c]
        for t in range(TR):
            row = jnp.concatenate([res[c, t : t + 1, :], res[c, 3 + t : 4 + t, :]], axis=1)
            row = row * fb[c, 4:5, :] * (1.0 / FOOT)
            for h, piece in enumerate(parts_of(row, 2)):
                piece = piece.astype(F32)
                for j in range(KIND):
                    value = jnp.broadcast_to(piece * kindhot[c, j : j + 1, :], (16, CHUNK)).astype(BF16)
                    value = jnp.concatenate([value] * FOOT, axis=1)
                    r = h * PER + j * LON
                    terms[t, r : r + 16, :] = mask[0:16] * value
                    terms[t, r + 16 : r + 32, :] = mask[16:32] * value
            got = lax.dot_general(terms[t], lathot[c, 0:LAT, :], NT, preferred_element_type=F32)
            total[t * PER : (t + 1) * PER, :] += got[0:PER] + got[PER:]

    loop(0, NLEV, scatter)
    ret_in[tile] = res[tile // 4]

    def force(i):
        t, h = i // 4, lax.rem(i, 4)
        rows = pl.ds(pl.multiple_of(h * 8, 8), 8)
        for w in range(LAT // 128):
            cols = slice(w * 128, (w + 1) * 128)
            sums = [
                total[pl.ds(pl.multiple_of(t * PER + j * LON + h * 8, 8), 8), cols] for j in range(KIND)
            ]
            for n in range(EXT):
                acc = sums[0] * kern_wide[n, 0:1, :]
                for j in range(1, KIND):
                    acc = acc + sums[j] * kern_wide[n, j : j + 1, :]
                x2[t, n, rows, cols] = acc

    loop(0, 4 * TR, force)
    stage_lon(x2, 2, 1, 9)
    lons.append(lon_copies(2))
    for copy in lons[2]:
        copy.start()

    loop(1, NTILE, ret_wait)
    pair_odd, odd = lax.rem(tile // 2, 2) == 1, lax.rem(tile, 2) == 1
    keep = lax.broadcasted_iota(I32, (8, 128), 0) < TR

    def regroup(i):
        halves = []
        for h in range(2):
            got = ret_in[2 * i + h]
            got = jnp.where(pair_odd, pltpu.roll(got, 5, 0), got)
            moved = pltpu.roll(got, CAP, 1)
            halves.append(jnp.where(odd, got, moved) if h else jnp.where(odd, moved, got))
        both = jnp.where(half, halves[0], halves[1])
        cols = pl.ds(pl.multiple_of(i * 128, 128), 128)
        for j, piece in enumerate(parts_of(jnp.where(keep, both, 0.0), 3)):
            spread[j * 8 : j * 8 + 8, cols] = piece.astype(F32)

    loop(0, NTILE // 2, regroup)
    back = jnp.concatenate([spread[...], jnp.zeros((8, SLOTS), F32)], axis=0).astype(BF16)
    back = jnp.dot(back, hot[...], preferred_element_type=F32)
    residual[...] = (back[0:8] + back[8:16] + back[16:24])[0:TR]

    finish_lon(2)
    sweep(x2, 2, True, 1, 9, put_in(x3))

    @pl.when(lev == NLEV - 1)
    def _():
        x3[:, 8] = blank

    stage_lon(x3, 3, 2, 8)
    lons.append(lon_copies(3))
    for copy in lons[3]:
        copy.start()
    finish_lon(3)

    def put_gradient(t, n, y):
        gradient[t, n - 2] = y

    sweep(x3, 3, True, 2, 8, put_gradient)

    for copies in lons + [lev_copies]:
        for copy in copies:
            copy.wait_send()
    loop(1, NTILE, lambda d: ids_copy(d).wait_send())
    loop(1, NTILE, lambda d: ret_copy(lax.rem(tile + d, NTILE)).wait_send())

    def parts_sent(c):
        for d in range(1, NLEV):
            part_copy(c, d).wait_send()

    loop(0, NLEV, parts_sent)


def store(a, b, a_out, b_out, sem):
    copies = [pltpu.make_async_copy(a, a_out, sem.at[0]), pltpu.make_async_copy(b, b_out, sem.at[1])]
    for copy in copies:
        copy.start()
    for copy in copies:
        copy.wait()


def body(conc, u_wind, v_wind, mixing, kernels, observed, obs_weight, column_tile, footprint, kernel_index):
    dma = pltpu.SemaphoreType.DMA
    anywhere, vmem = pl.BlockSpec(memory_space=pl.ANY), pl.BlockSpec(memory_space=pltpu.VMEM)
    ext = pltpu.VMEM((TR, EXT, LON, LAT), F32)
    shapes = (
        jax.ShapeDtypeStruct((TR, SND), F32),
        jax.ShapeDtypeStruct((TR, LV, LON, LAT), F32),
    )
    found = pl.pallas_call(
        kernel,
        out_shape=shapes,
        in_specs=[anywhere] * 4 + [vmem] * 6,
        out_specs=(vmem, vmem),
        scratch_shapes=[
            ext, ext, ext, ext,
            pltpu.VMEM((LV + 2, LON, LAT), F32),
            pltpu.VMEM((LV + 2, LON, LAT), F32),
            pltpu.VMEM((LV + 3, LON, LAT), F32),
            pltpu.VMEM((4, 2, 32, LAT), F32),
            pltpu.VMEM((4, 2, 32, LAT), F32),
            pltpu.VMEM((3, KIND, 128), F32),
            pltpu.VMEM((EXT, KIND, 128), F32),
            pltpu.VMEM((16, SND), F32),
            pltpu.VMEM((NTILE, 8, 128), F32),
            pltpu.VMEM((NTILE, 8, 128), F32),
            pltpu.VMEM((SLOTS, SND), BF16),
            pltpu.VMEM((NLEV, 8, CHUNK), F32),
            pltpu.VMEM((NLEV, KIND, CHUNK), F32),
            pltpu.VMEM((NLEV, 2 * LAT, LOOK), BF16),
            pltpu.VMEM((NLEV, LON, LOOK), F32),
            pltpu.VMEM((NLEV, LON, LOOK), BF16),
            pltpu.VMEM((24, SLOTS), F32),
            pltpu.VMEM((ROWS, 2 * LAT), BF16),
            pltpu.VMEM((ROWS, LOOK), F32),
            pltpu.VMEM((NLEV, 8, 128), F32),
            pltpu.VMEM((NLEV, NLEV, 8, 128), F32),
            pltpu.VMEM((NLEV, 8, 128), F32),
            pltpu.VMEM((NTILE, 8, 128), F32),
            pltpu.VMEM((TR, 2 * PER, LOOK), BF16),
            pltpu.VMEM((ROWS, LAT), F32),
            dma((4,)),
            dma((8,)), dma((8,)),
            dma((4, 2)), dma((4, 2)),
            dma((NTILE,)), dma((NTILE,)),
            dma((NLEV, NLEV)), dma((NLEV, NLEV)),
            dma((NTILE,)), dma((NTILE,)),
        ],
        compiler_params=pltpu.CompilerParams(
            collective_id=0, has_side_effects=True, vmem_limit_bytes=48 * 1024 * 1024
        ),
    )(
        conc, u_wind, v_wind, mixing, kernels, observed, obs_weight[None], column_tile.T, footprint.T, kernel_index[None]
    )
    return pl.pallas_call(
        store,
        out_shape=shapes,
        in_specs=[anywhere] * 2,
        out_specs=(anywhere, anywhere),
        scratch_shapes=[dma((2,))],
    )(*found)


def solution(mesh):
    placed = (
        P(None, "lev", "tile", None),
        P("lev", "tile", None),
        P("lev", "tile", None),
        P("lev", "tile", None),
        P(None, "lev"),
        P(None, "tile"),
        P("tile"),
        P("tile", None),
        P("tile", None),
        P("tile"),
    )
    return jax.shard_map(
        body,
        mesh=mesh,
        in_specs=placed,
        out_specs=(P(None, "tile"), P(None, "lev", "tile", None)),
        check_vma=False,
    )
```

time: 373 us -> 104 us (0.28)
  local copies, waits for them, and re-layouts: 121 us -> 9.74 us
  other arithmetic: 105 us -> 0 us
  Pallas kernels: 0 us -> 92.6 us
  starting transfers between devices: 80.3 us -> 0 us
  blocking collectives: 38.2 us -> 0 us
  waiting for transfers between devices: 19.3 us -> 0 us
  matrix products: 4.55 us -> 0 us
    pallas_call x0 -> x2, Pallas kernels: none -> 92.6 us  [the longest x1 64.2 us: body(): pl.pallas_call(kernel, out_shape=shapes, in_specs=[anywhere] * 4 + [vmem]...]
    scatter-add x1 -> x0, other arithmetic: 69.1 us -> none  [body(): summed = jnp.zeros((tracer_count, kind_count * col_count), jnp.float32).a...]
    ppermute x18 -> x0, starting transfers between devices: 55.8 us -> none  [the longest x8 30.5 us: padded_2(): before = lax.ppermute(last, axis, up)]
    reshape x4 -> x0, local copies, waits for them, and re-layouts: 53.6 us -> none  [the longest x1 27 us: body(): summed.reshape(tracer_count, kind_count, col_count)]
    gather x2 -> x0, local copies, waits for them, and re-layouts: 47.4 us -> none  [the longest x1 43.3 us: body(): jnp.take(profile_flat, flat_index.reshape(-1), axis=1)]
    psum x1 -> x0, blocking collectives: 27.5 us -> none  [body(): model_in = lax.psum(partial_value, 'lev') / foot_count]
    all_to_all x2 -> x0, starting transfers between devices: 24.6 us -> none  [the longest x1 15.8 us: body(): lax.all_to_all(model_in, 'tile', split_axis=1, concat_axis=1, tiled=True)]
    ppermute x18 -> x0, waiting for transfers between devices: 12.4 us -> none  [the longest x8 6.53 us: padded_2(): after = lax.ppermute(leading, axis, down)]
  transfers between devices with their start and end apart: 20 -> 0, of which waited for: 9 -> 0; matrix products, arithmetic and copies ran while one was open for 9% -> 0% of each run, Pallas kernels for 0% -> 0%
where the time goes in v2:
time: 104 us; the launch traced here: 103 us
  Pallas kernels  92.6 us (89%)
  local copies, waits for them, and re-layouts  9.74 us (9%)
    pallas_call x1, Pallas kernels, body(): pl.pallas_call(kernel, out_shape=shapes, in_specs=[anywhere] * 4 + [vmem]...  64.2 us
    pallas_call x1, Pallas kernels, body(): pl.pallas_call(store, out_shape=shapes, in_specs=[anywhere] * 2, out_spec...  28.4 us
    unnamed x24, local copies, waits for them, and re-layouts  9.74 us

profile of v2, /device:TPU:1, one launch (start us, length us, event | category | flops | bytes accessed | tf_op | source)
XLA Modules:
  0.0 103.0 jit_solution(4616211971698713488)
XLA Ops:
  0.6 0.0 copy-start.8
  0.6 0.7 copy-done.8
  1.3 0.0 copy-start
  1.3 1.2 %copy-done = f32[3,6,32,384]{3,2,1,0:T(8,128)S(1)} copy-done((f32[3,6,32,384]{3,2,1,0:T(8,128)S(1)}, f32[3,6,32,384]{3,2,1,0:T(8,128)}, u32[]{:S(2)}) %copy-start) | copy-done | bytes 884760
  2.5 0.0 copy-start.2
  2.5 1.0 copy-done.2
  3.5 0.0 copy-start.3
  3.5 1.0 copy-done.3
  4.4 0.0 copy-start.4
  4.4 1.0 copy-done.4
  5.4 0.0 copy-start.5
  5.4 0.7 copy-done.5
  6.1 0.0 copy-start.6
  6.1 0.7 copy-done.6
  6.8 0.0 copy-start.9
  6.8 0.7 copy-done.9
  7.5 0.0 copy-start.10
  7.5 0.7 copy-done.10
  8.2 0.0 copy-start.11
  8.2 0.7 copy-done.11
  8.9 64.2 %shard_map.113 = (f32[3,1024]{1,0:T(4,128)S(1)}, f32[3,6,32,384]{3,2,1,0:T(8,128)S(1)}) custom-call(f32[3,6,32,384]{3,2,1,0:T(8,128)S(1)} %copy-done, f32[6,32,384]{2,1,0:T(8,128)S(1)} %copy-done.2, f32[6,32,384]{2,1,0:T(8,128)S(1)} %copy-done.3, f32[6,32,384]{2,1,0:T(8,128)S(1)} %copy-done.4, f32[8,6]{1,0:T(8,128)S(1)} %copy-done.8, ...), custom_call_target="tpu_custom_call" | custom-call | tf_op jit(solution)/shard_map/pallas_call | solution.py:457
  73.1 0.0 copy-start.1
  73.1 0.9 copy-done.1
  74.0 0.0 copy-start.7
  74.0 0.6 copy-done.7
  74.6 28.4 %shard_map.114 = (f32[3,1024]{1,0:T(4,128)}, f32[3,6,32,384]{3,2,1,0:T(8,128)}) custom-call(f32[3,1024]{1,0:T(4,128)} %copy-done.7, f32[3,6,32,384]{3,2,1,0:T(8,128)} %copy-done.1), custom_call_target="tpu_custom_call" | custom-call | tf_op jit(solution)/shard_map/pallas_call | solution.py:502
Async XLA Ops:
  0.6 0.7 copy-start.8
  1.3 1.2 %copy-start = (f32[3,6,32,384]{3,2,1,0:T(8,128)S(1)}, f32[3,6,32,384]{3,2,1,0:T(8,128)}, u32[]{:S(2)}) copy-start(f32[3,6,32,384]{3,2,1,0:T(8,128)} %conc.1) | copy-start | bytes 2654212
  2.5 1.0 copy-start.2
  3.5 1.0 copy-start.3
  4.4 1.0 copy-start.4
  5.4 0.7 copy-start.5
  6.1 0.7 copy-start.6
  6.8 0.7 copy-start.9
  7.5 0.7 copy-start.10
  8.2 0.7 copy-start.11
  73.1 0.9 copy-start.1
  74.0 0.6 copy-start.7

commit v3 on v2

--- a/solution.py
+++ b/solution.py
@@ -41,12 +41,12 @@
 
 
 def kernel(
-    conc, u_in, v_in, k_in, kern, observed, weight, column, feet, kinds,
+    conc, u_in, v_in, k_in, kern_in, observed_in, weight_in, column_in, feet_in, kinds_in,
     residual, gradient,
-    x0, x1, x2, x3, u, v, k, lon_out, lon_in, kern_all, kern_wide, fields,
+    kern, observed, weight, column, feet, kinds, x0, x1, x2, x3, u, v, k, lon_out, lon_in, edge_u, diag_in, edge_y, kern_all, kern_wide, fields,
     ids_out, ids_in, hot, fb, kindhot, lathot, lonhot, lonbits, spread,
     e, picked, part_out, part_in, res, ret_in, terms, total,
-    local_sem, lev_ss, lev_rs, lon_ss, lon_rs, ids_ss, ids_rs, part_ss, part_rs, ret_ss, ret_rs,
+    local_sem, lev_ss, lev_rs, diag_ss, diag_rs, lon_ss, lon_rs, ids_ss, ids_rs, part_ss, part_rs, ret_ss, ret_rs,
 ):
     tile, lev = lax.axis_index("tile"), lax.axis_index("lev")
     east, west = lax.rem(tile + 1, NTILE), lax.rem(tile + NTILE - 1, NTILE)
@@ -62,8 +62,6 @@
     def greet(target):
         pl.semaphore_signal(barrier, inc=1, device_id=target, device_id_type=MESH)
 
-    loop(1, NLEV, lambda d: greet({"lev": lax.rem(lev + d, NLEV)}))
-    loop(1, NTILE, lambda d: greet({"tile": lax.rem(tile + d, NTILE)}))
     own = pl.ds(2, LV)
     loads = [
         pltpu.make_async_copy(conc, x0.at[:, own], local_sem.at[0]),
@@ -71,8 +69,16 @@
         pltpu.make_async_copy(v_in, v.at[pl.ds(1, LV)], local_sem.at[2]),
         pltpu.make_async_copy(k_in, k.at[own], local_sem.at[3]),
     ]
-    for copy in loads:
+    small = [(kern_in, kern), (observed_in, observed), (weight_in, weight), (column_in, column), (feet_in, feet), (kinds_in, kinds)]
+    smalls = [pltpu.make_async_copy(src, dst, local_sem.at[4 + n]) for n, (src, dst) in enumerate(small)]
+    for copy in smalls + loads:
         copy.start()
+    loop(1, NLEV, lambda d: greet({"lev": lax.rem(lev + d, NLEV)}))
+    loop(1, NTILE, lambda d: greet({"tile": lax.rem(tile + d, NTILE)}))
+    greet({"tile": west, "lev": below})
+    greet({"tile": west, "lev": above})
+    for copy in smalls:
+        copy.wait()
 
     half = lax.broadcasted_iota(I32, (8, 128), 1) < CAP
 
@@ -112,9 +118,12 @@
     x1[:, 0], x1[:, 9] = blank, blank
 
     def lon_copies(i):
+        rows = pl.ds(0, 48 if i else 32)
         return [
-            remote(lon_out.at[i, 0], lon_in.at[i, 0], lon_ss.at[i, 0], lon_rs.at[i, 0], {"tile": east}),
-            remote(lon_out.at[i, 1], lon_in.at[i, 1], lon_ss.at[i, 1], lon_rs.at[i, 1], {"tile": west}),
+            remote(
+                lon_out.at[i, side, rows], lon_in.at[i, side, rows], lon_ss.at[i, side], lon_rs.at[i, side], {"tile": to}
+            )
+            for side, to in enumerate((east, west))
         ]
 
     def stage_lon(x, i, low, high):
@@ -122,10 +131,21 @@
             for t in range(TR):
                 lon_out[i, 0, t * 8 + n - 1] = x[t, n, LON - 1]
                 lon_out[i, 1, t * 8 + n - 1] = x[t, n, 0]
-            if i < 2:
+                if i == 2:
+                    lon_out[i, 0, 23 + t * 8 + n] = x[t, n, LON - 2]
+                    lon_out[i, 1, 23 + t * 8 + n] = x[t, n, 1]
+            if i == 0:
                 lon_out[i, 0, 23 + n] = u[n - 1, LON - 1]
 
         loop(low, high, one)
+
+    def stage_winds(n):
+        lon_out[1, 0, 23 + n] = u[n - 1, LON - 2]
+        lon_out[1, 1, 23 + n] = u[n - 1, 0]
+        lon_out[1, 0, 31 + n] = v[n - 1, LON - 1]
+        lon_out[1, 1, 31 + n] = v[n - 1, 0]
+        lon_out[1, 0, 39 + n] = k[n, LON - 1]
+        lon_out[1, 1, 39 + n] = k[n, 0]
 
     def finish_lon(i):
         for copy in lons[i]:
@@ -133,13 +153,7 @@
 
         @pl.when(tile == NTILE - 1)
         def _():
-            lon_in[i, 1] = jnp.zeros((32, LAT), F32)
-
-        if i < 2:
-
-            @pl.when(tile == 0)
-            def _():
-                lon_in[i, 0, 24:32] = jnp.zeros((8, LAT), F32)
+            lon_in[i, 1] = jnp.zeros((48, LAT), F32)
 
     for copy in loads:
         copy.wait()
@@ -159,6 +173,12 @@
         remote(src, dst, lev_ss.at[n], lev_rs.at[n], {"lev": to}) for n, (src, dst, to) in enumerate(lev_moves)
     ]
     lons = [lon_copies(0)]
+    diag_copies = [
+        remote(
+            lon_out.at[0, 0, pl.ds(24, 8)], diag_in.at[n], diag_ss.at[n], diag_rs.at[n], {"tile": east, "lev": to}
+        )
+        for n, to in enumerate((above, below))
+    ]
 
     def ids_copy(d):
         peer = lax.rem(tile + d, NTILE)
@@ -168,10 +188,12 @@
         source = lax.rem(tile + NTILE - d, NTILE)
         remote(ids_out.at[source], ids_in.at[source], ids_ss.at[d], ids_rs.at[d], {"tile": source}).wait_recv()
 
-    pl.semaphore_wait(barrier, NTILE - 1 + NLEV - 1)
-    for copy in lons[0] + lev_copies:
+    pl.semaphore_wait(barrier, NTILE - 1 + NLEV - 1 + 2)
+    for copy in lons[0] + lev_copies[0:1]:
         copy.start()
     loop(1, NTILE, lambda d: ids_copy(d).start())
+    for copy in diag_copies + lev_copies[1:]:
+        copy.start()
 
     last_row = lax.broadcasted_iota(I32, (LON, LAT), 0) == LON - 1
     first_row = lax.broadcasted_iota(I32, (LON, LAT), 0) == 0
@@ -180,7 +202,7 @@
     def sweep(x, i, adjoint, low, high, put):
         def one(n):
             ul, kl, kb = u[n - 1], k[n], k[n - 1]
-            uw = jnp.where(first_row, lon_in[min(i, 1), 0, pl.ds(23 + n, 1), :], pltpu.roll(ul, 1, 0))
+            uw = jnp.where(first_row, edge_u[pl.ds(n - 1, 1), :], pltpu.roll(ul, 1, 0))
             vl = jnp.where(open_face, v[n - 1], 0.0)
             a, bw = jnp.maximum(ul, 0.0), jnp.minimum(uw, 0.0)
             p, q = jnp.maximum(vl, 0.0), jnp.minimum(vl, 0.0)
@@ -191,8 +213,9 @@
             for t in range(TR):
                 row = pl.ds(t * 8 + n - 1, 1)
                 c = x[t, n]
-                ce = jnp.where(last_row, lon_in[i, 1, row, :], pltpu.roll(c, LON - 1, 0))
-                cw = jnp.where(first_row, lon_in[i, 0, row, :], pltpu.roll(c, 1, 0))
+                edge_w, edge_e = (lon_in[i, 0, row, :], lon_in[i, 1, row, :]) if i < 3 else (edge_y[0, row, :], edge_y[1, row, :])
+                ce = jnp.where(last_row, edge_e, pltpu.roll(c, LON - 1, 0))
+                cw = jnp.where(first_row, edge_w, pltpu.roll(c, 1, 0))
                 cn = pltpu.roll(c, LAT - 1, 1)
                 vert = kl * (x[t, n + 1] - c) - kb * (c - x[t, n - 1])
                 if adjoint:
@@ -218,6 +241,12 @@
         k[0:2] = jnp.zeros((2, LON, LAT), F32)
 
     finish_lon(0)
+    edge_u[...] = lon_in[0, 0, 24:32]
+
+    @pl.when(tile == 0)
+    def _():
+        edge_u[...] = jnp.zeros((8, LAT), F32)
+
     sweep(x0, 0, False, 2, 8, put_in(x1))
     for t in range(TR):
         x1[t, 1] = k[1] * x0[t, 2]
@@ -227,24 +256,13 @@
     def _():
         x1[:, 8] = blank
 
-    for copy in lev_copies[1:]:
-        copy.wait_recv()
     stage_lon(x1, 1, 1, 9)
+    loop(2, 8, stage_winds)
+    lon_out[1, 0, 40] = k[1, LON - 1]
+    lon_out[1, 1, 40] = k[1, 0]
     lons.append(lon_copies(1))
     for copy in lons[1]:
         copy.start()
-
-    @pl.when(lev == 0)
-    def _():
-        kern_all[1] = jnp.zeros((KIND, 128), F32)
-
-    @pl.when(lev == NLEV - 1)
-    def _():
-        kern_all[2] = jnp.zeros((KIND, 128), F32)
-
-    for n in range(EXT):
-        which, col = (1, 4 + n) if n < 2 else (0, n - 2) if n < 8 else (2, n - 8)
-        kern_wide[n] = jnp.broadcast_to(kern_all[which, :, col : col + 1], (KIND, 128))
 
     loop(1, NTILE, ids_wait)
 
@@ -269,6 +287,27 @@
 
     loop(0, NLEV, unpack)
 
+    for copy in lev_copies[1:] + diag_copies:
+        copy.wait_recv()
+    edge_u[0:1] = diag_in[0, 6:7]
+    edge_u[7:8] = diag_in[1, 1:2]
+
+    @pl.when(tile == 0)
+    def _():
+        edge_u[...] = jnp.zeros((8, LAT), F32)
+
+    @pl.when(lev == 0)
+    def _():
+        kern_all[1] = jnp.zeros((KIND, 128), F32)
+
+    @pl.when(lev == NLEV - 1)
+    def _():
+        kern_all[2] = jnp.zeros((KIND, 128), F32)
+
+    for n in range(EXT):
+        which, col = (1, 4 + n) if n < 2 else (0, n - 2) if n < 8 else (2, n - 8)
+        kern_wide[n] = jnp.broadcast_to(kern_all[which, :, col : col + 1], (KIND, 128))
+
     finish_lon(1)
     sweep(x1, 1, False, 1, 9, put_in(x2))
     for t in range(TR):
@@ -414,18 +453,38 @@
     def _():
         x3[:, 8] = blank
 
-    stage_lon(x3, 3, 2, 8)
-    lons.append(lon_copies(3))
-    for copy in lons[3]:
-        copy.start()
-    finish_lon(3)
+    lane = lax.broadcasted_iota(I32, (8, LAT), 1) < LAT - 1
+    here_u = edge_u[...]
+    east_u = jnp.concatenate([u[n, LON - 1 : LON, :] for n in range(8)], axis=0)
+    for side in range(2):
+        wind = lon_in[1, side, 24:32, :]
+        right, left = (here_u, wind) if side == 0 else (wind, east_u)
+        north = jnp.where(lane, lon_in[1, side, 32:40, :], 0.0)
+        up_k = lon_in[1, side, 40:48, :]
+        low_k = pltpu.roll(up_k, 1, 0)
+        a, bw = jnp.maximum(right, 0.0), jnp.minimum(left, 0.0)
+        p, qs = jnp.maximum(north, 0.0), pltpu.roll(jnp.minimum(north, 0.0), 1, 1)
+        for t in range(TR):
+            c = lon_in[2, side, t * 8 : t * 8 + 8, :]
+            far = lon_in[2, side, 24 + t * 8 : 32 + t * 8, :]
+            near = jnp.concatenate([x2[t, n, side * (LON - 1) : side * (LON - 1) + 1, :] for n in range(1, 9)], axis=0)
+            ce, cw = (near, far) if side == 0 else (far, near)
+            cn, cs = pltpu.roll(c, LAT - 1, 1), pltpu.roll(c, 1, 1)
+            vert = up_k * (pltpu.roll(c, 7, 0) - c) - low_k * (c - pltpu.roll(c, 1, 0))
+            edge_y[side, t * 8 : t * 8 + 8, :] = (
+                c + (a * (ce - c) + bw * (c - cw)) + (p * (cn - c) + qs * (c - cs)) + vert
+            )
+
+    @pl.when(tile == NTILE - 1)
+    def _():
+        edge_y[1] = jnp.zeros((24, LAT), F32)
 
     def put_gradient(t, n, y):
         gradient[t, n - 2] = y
 
     sweep(x3, 3, True, 2, 8, put_gradient)
 
-    for copies in lons + [lev_copies]:
+    for copies in lons + [lev_copies, diag_copies]:
         for copy in copies:
             copy.wait_send()
     loop(1, NTILE, lambda d: ids_copy(d).wait_send())
@@ -438,17 +497,23 @@
     loop(0, NLEV, parts_sent)
 
 
-def store(a, b, a_out, b_out, sem):
-    copies = [pltpu.make_async_copy(a, a_out, sem.at[0]), pltpu.make_async_copy(b, b_out, sem.at[1])]
-    for copy in copies:
+def store(a, b, a_out, b_out, a_held, b_held, in_sem, out_sem):
+    into = [pltpu.make_async_copy(b.at[t], b_held.at[t], in_sem.at[t]) for t in range(TR)]
+    out = [pltpu.make_async_copy(b_held.at[t], b_out.at[t], out_sem.at[t]) for t in range(TR)]
+    into.append(pltpu.make_async_copy(a, a_held, in_sem.at[TR]))
+    out.append(pltpu.make_async_copy(a_held, a_out, out_sem.at[TR]))
+    for copy in into:
         copy.start()
-    for copy in copies:
+    for got, put in zip(into, out):
+        got.wait()
+        put.start()
+    for copy in out:
         copy.wait()
 
 
 def body(conc, u_wind, v_wind, mixing, kernels, observed, obs_weight, column_tile, footprint, kernel_index):
     dma = pltpu.SemaphoreType.DMA
-    anywhere, vmem = pl.BlockSpec(memory_space=pl.ANY), pl.BlockSpec(memory_space=pltpu.VMEM)
+    hbm, vmem = pl.BlockSpec(memory_space=pl.ANY), pl.BlockSpec(memory_space=pltpu.VMEM)
     ext = pltpu.VMEM((TR, EXT, LON, LAT), F32)
     shapes = (
         jax.ShapeDtypeStruct((TR, SND), F32),
@@ -457,15 +522,24 @@
     found = pl.pallas_call(
         kernel,
         out_shape=shapes,
-        in_specs=[anywhere] * 4 + [vmem] * 6,
+        in_specs=[hbm] * 10,
         out_specs=(vmem, vmem),
         scratch_shapes=[
+            pltpu.VMEM((KIND, LV), F32),
+            pltpu.VMEM((TR, SND), F32),
+            pltpu.VMEM((1, SND), F32),
+            pltpu.VMEM((1, SND), I32),
+            pltpu.VMEM((FOOT, SND), I32),
+            pltpu.VMEM((1, SND), I32),
             ext, ext, ext, ext,
             pltpu.VMEM((LV + 2, LON, LAT), F32),
             pltpu.VMEM((LV + 2, LON, LAT), F32),
             pltpu.VMEM((LV + 3, LON, LAT), F32),
-            pltpu.VMEM((4, 2, 32, LAT), F32),
-            pltpu.VMEM((4, 2, 32, LAT), F32),
+            pltpu.VMEM((3, 2, 48, LAT), F32),
+            pltpu.VMEM((3, 2, 48, LAT), F32),
+            pltpu.VMEM((8, LAT), F32),
+            pltpu.VMEM((2, 8, LAT), F32),
+            pltpu.VMEM((2, 24, LAT), F32),
             pltpu.VMEM((3, KIND, 128), F32),
             pltpu.VMEM((EXT, KIND, 128), F32),
             pltpu.VMEM((16, SND), F32),
@@ -486,15 +560,16 @@
             pltpu.VMEM((NTILE, 8, 128), F32),
             pltpu.VMEM((TR, 2 * PER, LOOK), BF16),
             pltpu.VMEM((ROWS, LAT), F32),
-            dma((4,)),
+            dma((10,)),
             dma((8,)), dma((8,)),
-            dma((4, 2)), dma((4, 2)),
+            dma((2,)), dma((2,)),
+            dma((3, 2)), dma((3, 2)),
             dma((NTILE,)), dma((NTILE,)),
             dma((NLEV, NLEV)), dma((NLEV, NLEV)),
             dma((NTILE,)), dma((NTILE,)),
         ],
         compiler_params=pltpu.CompilerParams(
-            collective_id=0, has_side_effects=True, vmem_limit_bytes=48 * 1024 * 1024
+            collective_id=0, has_side_effects=True, vmem_limit_bytes=60 * 1024 * 1024
         ),
     )(
         conc, u_wind, v_wind, mixing, kernels, observed, obs_weight[None], column_tile.T, footprint.T, kernel_index[None]
@@ -502,9 +577,15 @@
     return pl.pallas_call(
         store,
         out_shape=shapes,
-        in_specs=[anywhere] * 2,
-        out_specs=(anywhere, anywhere),
-        scratch_shapes=[dma((2,))],
+        in_specs=[hbm] * 2,
+        out_specs=(hbm, hbm),
+        scratch_shapes=[
+            pltpu.VMEM((TR, SND), F32),
+            pltpu.VMEM((TR, LV, LON, LAT), F32),
+            dma((TR + 1,)),
+            dma((TR + 1,)),
+        ],
+        compiler_params=pltpu.CompilerParams(vmem_limit_bytes=60 * 1024 * 1024),
     )(*found)
 
 

time: 104 us -> 65 us (0.62)
  Pallas kernels: 92.6 us -> 64.3 us
  local copies, waits for them, and re-layouts: 9.74 us -> 0 us
    pallas_call x2, Pallas kernels: 92.6 us -> 64.3 us  [the longest x1 62.3 us: body(): pl.pallas_call(kernel, out_shape=shapes, in_specs=[hbm] * 10, out_specs=(...]
    unnamed x24 -> x0, local copies, waits for them, and re-layouts: 9.74 us -> none
where the time goes in v3:
time: 65 us; the launch traced here: 64.9 us
  Pallas kernels  64.3 us (99%)
    pallas_call x1, Pallas kernels, body(): pl.pallas_call(kernel, out_shape=shapes, in_specs=[hbm] * 10, out_specs=(...  62.3 us
    pallas_call x1, Pallas kernels, body(): pl.pallas_call(store, out_shape=shapes, in_specs=[hbm] * 2, out_specs=(hb...  1.94 us

profile of v3, /device:TPU:1, one launch (start us, length us, event | category | flops | bytes accessed | tf_op | source)
XLA Modules:
  0.0 64.9 jit_solution(6881331977649927949)
XLA Ops:
  0.6 62.3 %shard_map.113 = (f32[3,1024]{1,0:T(4,128)}, f32[3,6,32,384]{3,2,1,0:T(8,128)}) custom-call(f32[3,6,32,384]{3,2,1,0:T(8,128)} %conc.1, f32[6,32,384]{2,1,0:T(8,128)} %u_in.1, f32[6,32,384]{2,1,0:T(8,128)} %v_in.1, f32[6,32,384]{2,1,0:T(8,128)} %k_in.1, f32[8,6]{1,0:T(8,128)} %kern_in.1, f32[3,1024]{1,0:T(4,128)} %observed_in.1, f32[1,1024]{1,0:T(1,128)} %bitcast.5, ...), custom_call_target="tpu_custom_call" | custom-call | tf_op jit(solution)/shard_map/pallas_call | solution.py:522
  63.0 1.9 %shard_map.114 = (f32[3,1024]{1,0:T(4,128)}, f32[3,6,32,384]{3,2,1,0:T(8,128)}) custom-call(f32[3,1024]{1,0:T(4,128)} %get-tuple-element.4.a, f32[3,6,32,384]{3,2,1,0:T(8,128)} %get-tuple-element.5.b), custom_call_target="tpu_custom_call" | custom-call | tf_op jit(solution)/shard_map/pallas_call | solution.py:577

commit v4 on v3

--- a/solution.py
+++ b/solution.py
@@ -32,6 +32,11 @@
     return (lax.broadcasted_iota(I32, shape, 0) + base == index).astype(F32)
 
 
+def unrolled(low, high, body):
+    for i in range(low, high):
+        body(i)
+
+
 def loop(low, high, body):
     def step(i, carry):
         body(i)
@@ -44,7 +49,7 @@
     conc, u_in, v_in, k_in, kern_in, observed_in, weight_in, column_in, feet_in, kinds_in,
     residual, gradient,
     kern, observed, weight, column, feet, kinds, x0, x1, x2, x3, u, v, k, lon_out, lon_in, edge_u, diag_in, edge_y, kern_all, kern_wide, fields,
-    ids_out, ids_in, hot, fb, kindhot, lathot, lonhot, lonbits, spread,
+    ids_out, ids_in, hot, fb, kindhot, code, lathot, lonhot, cellhot, spread,
     e, picked, part_out, part_in, res, ret_in, terms, total,
     local_sem, lev_ss, lev_rs, diag_ss, diag_rs, lon_ss, lon_rs, ids_ss, ids_rs, part_ss, part_rs, ret_ss, ret_rs,
 ):
@@ -62,6 +67,10 @@
     def greet(target):
         pl.semaphore_signal(barrier, inc=1, device_id=target, device_id_type=MESH)
 
+    loop(1, NLEV, lambda d: greet({"lev": lax.rem(lev + d, NLEV)}))
+    loop(1, NTILE, lambda d: greet({"tile": lax.rem(tile + d, NTILE)}))
+    greet({"tile": west, "lev": below})
+    greet({"tile": west, "lev": above})
     own = pl.ds(2, LV)
     loads = [
         pltpu.make_async_copy(conc, x0.at[:, own], local_sem.at[0]),
@@ -73,10 +82,6 @@
     smalls = [pltpu.make_async_copy(src, dst, local_sem.at[4 + n]) for n, (src, dst) in enumerate(small)]
     for copy in smalls + loads:
         copy.start()
-    loop(1, NLEV, lambda d: greet({"lev": lax.rem(lev + d, NLEV)}))
-    loop(1, NTILE, lambda d: greet({"tile": lax.rem(tile + d, NTILE)}))
-    greet({"tile": west, "lev": below})
-    greet({"tile": west, "lev": above})
     for copy in smalls:
         copy.wait()
 
@@ -137,7 +142,7 @@
             if i == 0:
                 lon_out[i, 0, 23 + n] = u[n - 1, LON - 1]
 
-        loop(low, high, one)
+        unrolled(low, high, one)
 
     def stage_winds(n):
         lon_out[1, 0, 23 + n] = u[n - 1, LON - 2]
@@ -184,8 +189,8 @@
         peer = lax.rem(tile + d, NTILE)
         return remote(ids_out.at[peer], ids_in.at[tile], ids_ss.at[d], ids_rs.at[d], {"tile": peer})
 
-    def ids_wait(d):
-        source = lax.rem(tile + NTILE - d, NTILE)
+    def ids_wait(source):
+        d = lax.rem(tile + NTILE - source, NTILE)
         remote(ids_out.at[source], ids_in.at[source], ids_ss.at[d], ids_rs.at[d], {"tile": source}).wait_recv()
 
     pl.semaphore_wait(barrier, NTILE - 1 + NLEV - 1 + 2)
@@ -264,9 +269,15 @@
     for copy in lons[1]:
         copy.start()
 
-    loop(1, NTILE, ids_wait)
-
-    def unpack(c):
+    def unpack(i):
+        c = lax.rem(tile // 4 + i, NLEV)
+        for n in range(4):
+            source = c * 4 + n
+
+            @pl.when(source != tile)
+            def _():
+                ids_wait(source)
+
         left, right = [], []
         for h in range(2):
             a, b = ids_in[c * 4 + h * 2], ids_in[c * 4 + h * 2 + 1]
@@ -275,15 +286,15 @@
         ga, gb = jnp.concatenate(left, axis=1), jnp.concatenate(right, axis=1)
         fb[c] = gb
         ga = ga.astype(I32)
-        kindhot[c] = onehot(KIND, gb[0:1, :].astype(I32))
+        kind = gb[0:1, :].astype(I32)
+        kindhot[c] = onehot(KIND, kind)
+        code[c] = kind * LON + ga[4:8, :]
         for j in range(FOOT):
             cols = slice(j * CHUNK, (j + 1) * CHUNK)
             lat = onehot(LAT, ga[j : j + 1, :]).astype(BF16)
             lathot[c, 0:LAT, cols] = lat
             lathot[c, LAT : 2 * LAT, cols] = lat
-            lon = onehot(LON, ga[4 + j : 5 + j, :])
-            lonhot[c, :, cols] = lon
-            lonbits[c, :, cols] = lon.astype(BF16)
+            lonhot[c, :, cols] = onehot(LON, ga[4 + j : 5 + j, :])
 
     loop(0, NLEV, unpack)
 
@@ -343,6 +354,8 @@
 
     def gather(c):
         picked[...] = jnp.dot(e[...], lathot[c], preferred_element_type=F32)
+        for j in range(FOOT):
+            cellhot[c, :, j * CHUNK : (j + 1) * CHUNK] = onehot(PER, code[c, j : j + 1, :]).astype(BF16)
         mask = lonhot[c]
         for t in range(TR):
             acc = jnp.zeros((LON, CHUNK), F32)
@@ -370,9 +383,9 @@
         source = lax.rem(tile + NTILE - d, NTILE)
         remote(res.at[source // 4], ret_in.at[source], ret_ss.at[d], ret_rs.at[d], {"tile": source}).wait_recv()
 
-    total[...] = jnp.zeros((ROWS, LAT), F32)
-
-    def scatter(c):
+    total[...] = jnp.zeros((PER, 2 * TR * LAT), F32)
+
+    def settle(c):
         for d in range(1, NLEV):
             part_wait(c, d)
         model = part_in[0, c]
@@ -387,43 +400,51 @@
             def _():
                 ret_copy(peer).start()
 
-        mask = lonbits[c]
+    ahead = 3
+    loop(0, ahead, settle)
+
+    def scatter(c):
+        @pl.when(c < NLEV - ahead)
+        def _():
+            settle(c + ahead)
+
         for t in range(TR):
             row = jnp.concatenate([res[c, t : t + 1, :], res[c, 3 + t : 4 + t, :]], axis=1)
             row = row * fb[c, 4:5, :] * (1.0 / FOOT)
             for h, piece in enumerate(parts_of(row, 2)):
-                piece = piece.astype(F32)
-                for j in range(KIND):
-                    value = jnp.broadcast_to(piece * kindhot[c, j : j + 1, :], (16, CHUNK)).astype(BF16)
-                    value = jnp.concatenate([value] * FOOT, axis=1)
-                    r = h * PER + j * LON
-                    terms[t, r : r + 16, :] = mask[0:16] * value
-                    terms[t, r + 16 : r + 32, :] = mask[16:32] * value
-            got = lax.dot_general(terms[t], lathot[c, 0:LAT, :], NT, preferred_element_type=F32)
-            total[t * PER : (t + 1) * PER, :] += got[0:PER] + got[PER:]
+                value = jnp.broadcast_to(piece.astype(F32), (16, CHUNK)).astype(BF16)
+                value = jnp.concatenate([value] * FOOT, axis=1)
+                for r in range(0, LAT, 16):
+                    terms[t, h * LAT + r : h * LAT + r + 16, :] = lathot[c, r : r + 16, :] * value
+            cols = slice(t * 2 * LAT, (t + 1) * 2 * LAT)
+            total[:, cols] += lax.dot_general(cellhot[c], terms[t], NT, preferred_element_type=F32)
 
     loop(0, NLEV, scatter)
     ret_in[tile] = res[tile // 4]
 
-    def force(i):
-        t, h = i // 4, lax.rem(i, 4)
+    def force(h):
         rows = pl.ds(pl.multiple_of(h * 8, 8), 8)
-        for w in range(LAT // 128):
-            cols = slice(w * 128, (w + 1) * 128)
-            sums = [
-                total[pl.ds(pl.multiple_of(t * PER + j * LON + h * 8, 8), 8), cols] for j in range(KIND)
-            ]
-            for n in range(EXT):
-                acc = sums[0] * kern_wide[n, 0:1, :]
-                for j in range(1, KIND):
-                    acc = acc + sums[j] * kern_wide[n, j : j + 1, :]
-                x2[t, n, rows, cols] = acc
-
-    loop(0, 4 * TR, force)
+        for t in range(TR):
+            for w in range(LAT // 128):
+                cols = slice(w * 128, (w + 1) * 128)
+                start_high = t * 2 * LAT + w * 128
+                high, low = slice(start_high, start_high + 128), slice(start_high + LAT, start_high + LAT + 128)
+                sums = []
+                for j in range(KIND):
+                    cells = pl.ds(pl.multiple_of(j * LON + h * 8, 8), 8)
+                    sums.append(total[cells, high] + total[cells, low])
+                for n in range(EXT):
+                    acc = sums[0] * kern_wide[n, 0:1, :]
+                    for j in range(1, KIND):
+                        acc = acc + sums[j] * kern_wide[n, j : j + 1, :]
+                    x2[t, n, rows, cols] = acc
+
+    loop(0, 2, lambda i: force(i * 3))
     stage_lon(x2, 2, 1, 9)
     lons.append(lon_copies(2))
     for copy in lons[2]:
         copy.start()
+    loop(1, 3, force)
 
     loop(1, NTILE, ret_wait)
     pair_odd, odd = lax.rem(tile // 2, 2) == 1, lax.rem(tile, 2) == 1
@@ -487,8 +508,8 @@
     for copies in lons + [lev_copies, diag_copies]:
         for copy in copies:
             copy.wait_send()
-    loop(1, NTILE, lambda d: ids_copy(d).wait_send())
-    loop(1, NTILE, lambda d: ret_copy(lax.rem(tile + d, NTILE)).wait_send())
+    unrolled(1, NTILE, lambda d: ids_copy(d).wait_send())
+    unrolled(1, NTILE, lambda d: ret_copy(lax.rem(tile + d, NTILE)).wait_send())
 
     def parts_sent(c):
         for d in range(1, NLEV):
@@ -548,9 +569,10 @@
             pltpu.VMEM((SLOTS, SND), BF16),
             pltpu.VMEM((NLEV, 8, CHUNK), F32),
             pltpu.VMEM((NLEV, KIND, CHUNK), F32),
+            pltpu.VMEM((NLEV, FOOT, CHUNK), I32),
             pltpu.VMEM((NLEV, 2 * LAT, LOOK), BF16),
             pltpu.VMEM((NLEV, LON, LOOK), F32),
-            pltpu.VMEM((NLEV, LON, LOOK), BF16),
+            pltpu.VMEM((NLEV, PER, LOOK), BF16),
             pltpu.VMEM((24, SLOTS), F32),
             pltpu.VMEM((ROWS, 2 * LAT), BF16),
             pltpu.VMEM((ROWS, LOOK), F32),
@@ -558,8 +580,8 @@
             pltpu.VMEM((NLEV, NLEV, 8, 128), F32),
             pltpu.VMEM((NLEV, 8, 128), F32),
             pltpu.VMEM((NTILE, 8, 128), F32),
-            pltpu.VMEM((TR, 2 * PER, LOOK), BF16),
-            pltpu.VMEM((ROWS, LAT), F32),
+            pltpu.VMEM((TR, 2 * LAT, LOOK), BF16),
+            pltpu.VMEM((PER, 2 * TR * LAT), F32),
             dma((10,)),
             dma((8,)), dma((8,)),
             dma((2,)), dma((2,)),

time: 65 us -> 62.5 us (0.962)
  Pallas kernels: 64.3 us -> 61.7 us
    pallas_call x1, Pallas kernels: 62.3 us -> 59.8 us  [body(): pl.pallas_call(kernel, out_shape=shapes, in_specs=[hbm] * 10, out_specs=(...]
where the time goes in v4:
time: 62.5 us; the launch traced here: 62.3 us
  Pallas kernels  61.7 us (99%)
  between operations  0.64 us (1%)
    pallas_call x1, Pallas kernels, body(): pl.pallas_call(kernel, out_shape=shapes, in_specs=[hbm] * 10, out_specs=(...  59.8 us
    pallas_call x1, Pallas kernels, body(): pl.pallas_call(store, out_shape=shapes, in_specs=[hbm] * 2, out_specs=(hb...  1.94 us

profile of v4, /device:TPU:1, one launch (start us, length us, event | category | flops | bytes accessed | tf_op | source)
XLA Modules:
  0.0 62.3 jit_solution(13180693191243044939)
XLA Ops:
  0.6 59.8 %shard_map.113 = (f32[3,1024]{1,0:T(4,128)}, f32[3,6,32,384]{3,2,1,0:T(8,128)}) custom-call(f32[3,6,32,384]{3,2,1,0:T(8,128)} %conc.1, f32[6,32,384]{2,1,0:T(8,128)} %u_in.1, f32[6,32,384]{2,1,0:T(8,128)} %v_in.1, f32[6,32,384]{2,1,0:T(8,128)} %k_in.1, f32[8,6]{1,0:T(8,128)} %kern_in.1, f32[3,1024]{1,0:T(4,128)} %observed_in.1, f32[1,1024]{1,0:T(1,128)} %bitcast.5, ...), custom_call_target="tpu_custom_call" | custom-call | tf_op jit(solution)/shard_map/pallas_call | solution.py:543
  60.4 1.9 %shard_map.114 = (f32[3,1024]{1,0:T(4,128)}, f32[3,6,32,384]{3,2,1,0:T(8,128)}) custom-call(f32[3,1024]{1,0:T(4,128)} %get-tuple-element.4.a, f32[3,6,32,384]{3,2,1,0:T(8,128)} %get-tuple-element.5.b), custom_call_target="tpu_custom_call" | custom-call | tf_op jit(solution)/shard_map/pallas_call | solution.py:599

commit v5 on v4

--- a/solution.py
+++ b/solution.py
@@ -218,9 +218,11 @@
             for t in range(TR):
                 row = pl.ds(t * 8 + n - 1, 1)
                 c = x[t, n]
-                edge_w, edge_e = (lon_in[i, 0, row, :], lon_in[i, 1, row, :]) if i < 3 else (edge_y[0, row, :], edge_y[1, row, :])
-                ce = jnp.where(last_row, edge_e, pltpu.roll(c, LON - 1, 0))
-                cw = jnp.where(first_row, edge_w, pltpu.roll(c, 1, 0))
+                ce, cw = pltpu.roll(c, LON - 1, 0), pltpu.roll(c, 1, 0)
+                if i != 2:
+                    edges = edge_y if i == 3 else lon_in.at[i]
+                    ce = jnp.where(last_row, edges[1, row, :], ce)
+                    cw = jnp.where(first_row, edges[0, row, :], cw)
                 cn = pltpu.roll(c, LAT - 1, 1)
                 vert = kl * (x[t, n + 1] - c) - kb * (c - x[t, n - 1])
                 if adjoint:
@@ -446,6 +448,8 @@
         copy.start()
     loop(1, 3, force)
 
+    sweep(x2, 2, True, 1, 9, put_in(x3))
+
     loop(1, NTILE, ret_wait)
     pair_odd, odd = lax.rem(tile // 2, 2) == 1, lax.rem(tile, 2) == 1
     keep = lax.broadcasted_iota(I32, (8, 128), 0) < TR
@@ -468,12 +472,6 @@
     residual[...] = (back[0:8] + back[8:16] + back[16:24])[0:TR]
 
     finish_lon(2)
-    sweep(x2, 2, True, 1, 9, put_in(x3))
-
-    @pl.when(lev == NLEV - 1)
-    def _():
-        x3[:, 8] = blank
-
     lane = lax.broadcasted_iota(I32, (8, LAT), 1) < LAT - 1
     here_u = edge_u[...]
     east_u = jnp.concatenate([u[n, LON - 1 : LON, :] for n in range(8)], axis=0)
@@ -495,6 +493,35 @@
             edge_y[side, t * 8 : t * 8 + 8, :] = (
                 c + (a * (ce - c) + bw * (c - cw)) + (p * (cn - c) + qs * (c - cs)) + vert
             )
+
+    top, bottom = lax.broadcasted_iota(I32, (8, LAT), 0) == 7, lax.broadcasted_iota(I32, (8, LAT), 0) == 0
+
+    def column(ref, at, low=0):
+        return jnp.concatenate([ref[n, at : at + 1, :] for n in range(low, low + 8)], axis=0)
+
+    for side in range(2):
+        at = side * (LON - 1)
+        right, left = (column(u, 0), here_u) if side == 0 else (east_u, column(u, LON - 2))
+        north = jnp.where(lane, column(v, at), 0.0)
+        up_k, low_k = column(k, at, 1), column(k, at)
+        a, bw = jnp.maximum(right, 0.0), jnp.minimum(left, 0.0)
+        p, qs = jnp.maximum(north, 0.0), pltpu.roll(jnp.minimum(north, 0.0), 1, 1)
+        for t in range(TR):
+            c = lon_out[2, 1 - side, t * 8 : t * 8 + 8, :]
+            near = lon_out[2, 1 - side, 24 + t * 8 : 32 + t * 8, :]
+            far = lon_in[2, side, t * 8 : t * 8 + 8, :]
+            ce, cw = (near, far) if side == 0 else (far, near)
+            cn, cs = pltpu.roll(c, LAT - 1, 1), pltpu.roll(c, 1, 1)
+            up = jnp.where(top, x2[t, 9, at : at + 1, :], pltpu.roll(c, 7, 0))
+            low = jnp.where(bottom, x2[t, 0, at : at + 1, :], pltpu.roll(c, 1, 0))
+            vert = up_k * (up - c) - low_k * (c - low)
+            y = c + (a * (ce - c) + bw * (c - cw)) + (p * (cn - c) + qs * (c - cs)) + vert
+            for n in range(8):
+                x3[t, n + 1, at : at + 1, :] = y[n : n + 1, :]
+
+    @pl.when(lev == NLEV - 1)
+    def _():
+        x3[:, 8] = blank
 
     @pl.when(tile == NTILE - 1)
     def _():

time: 62.5 us -> 61.7 us (0.987)
  Pallas kernels: 61.7 us -> 61 us
    pallas_call x1, Pallas kernels: 59.8 us -> 59 us  [body(): pl.pallas_call(kernel, out_shape=shapes, in_specs=[hbm] * 10, out_specs=(...]
where the time goes in v5:
time: 61.7 us; the launch traced here: 61.6 us
  Pallas kernels  61 us (99%)
  between operations  0.64 us (1%)
    pallas_call x1, Pallas kernels, body(): pl.pallas_call(kernel, out_shape=shapes, in_specs=[hbm] * 10, out_specs=(...  59 us
    pallas_call x1, Pallas kernels, body(): pl.pallas_call(store, out_shape=shapes, in_specs=[hbm] * 2, out_specs=(hb...  1.94 us

profile of v5, /device:TPU:1, one launch (start us, length us, event | category | flops | bytes accessed | tf_op | source)
XLA Modules:
  0.0 61.6 jit_solution(7758386599359682615)
XLA Ops:
  0.6 59.0 %shard_map.113 = (f32[3,1024]{1,0:T(4,128)}, f32[3,6,32,384]{3,2,1,0:T(8,128)}) custom-call(f32[3,6,32,384]{3,2,1,0:T(8,128)} %conc.1, f32[6,32,384]{2,1,0:T(8,128)} %u_in.1, f32[6,32,384]{2,1,0:T(8,128)} %v_in.1, f32[6,32,384]{2,1,0:T(8,128)} %k_in.1, f32[8,6]{1,0:T(8,128)} %kern_in.1, f32[3,1024]{1,0:T(4,128)} %observed_in.1, f32[1,1024]{1,0:T(1,128)} %bitcast.5, ...), custom_call_target="tpu_custom_call" | custom-call | tf_op jit(solution)/shard_map/pallas_call | solution.py:570
  59.7 1.9 %shard_map.114 = (f32[3,1024]{1,0:T(4,128)}, f32[3,6,32,384]{3,2,1,0:T(8,128)}) custom-call(f32[3,1024]{1,0:T(4,128)} %get-tuple-element.4.a, f32[3,6,32,384]{3,2,1,0:T(8,128)} %get-tuple-element.5.b), custom_call_target="tpu_custom_call" | custom-call | tf_op jit(solution)/shard_map/pallas_call | solution.py:626

commit v6 on v5

--- a/solution.py
+++ b/solution.py
@@ -471,6 +471,16 @@
     back = jnp.dot(back, hot[...], preferred_element_type=F32)
     residual[...] = (back[0:8] + back[8:16] + back[16:24])[0:TR]
 
+    for copies in lons[0:2] + [lev_copies, diag_copies]:
+        for copy in copies:
+            copy.wait_send()
+    unrolled(1, NTILE, lambda d: ids_copy(d).wait_send())
+
+    def parts_sent(c):
+        for d in range(1, NLEV):
+            part_copy(c, d).wait_send()
+
+    loop(0, NLEV, parts_sent)
     finish_lon(2)
     lane = lax.broadcasted_iota(I32, (8, LAT), 1) < LAT - 1
     here_u = edge_u[...]
@@ -532,17 +542,9 @@
 
     sweep(x3, 3, True, 2, 8, put_gradient)
 
-    for copies in lons + [lev_copies, diag_copies]:
-        for copy in copies:
-            copy.wait_send()
-    unrolled(1, NTILE, lambda d: ids_copy(d).wait_send())
+    for copy in lons[2]:
+        copy.wait_send()
     unrolled(1, NTILE, lambda d: ret_copy(lax.rem(tile + d, NTILE)).wait_send())
-
-    def parts_sent(c):
-        for d in range(1, NLEV):
-            part_copy(c, d).wait_send()
-
-    loop(0, NLEV, parts_sent)
 
 
 def store(a, b, a_out, b_out, a_held, b_held, in_sem, out_sem):

time: 61.7 us -> 61.7 us (level)
  no operation moved by 1% of the time
where the time goes in v6:
time: 61.7 us; the launch traced here: 61.6 us
  Pallas kernels  61 us (99%)
  between operations  0.64 us (1%)
    pallas_call x1, Pallas kernels, body(): pl.pallas_call(kernel, out_shape=shapes, in_specs=[hbm] * 10, out_specs=(...  59 us
    pallas_call x1, Pallas kernels, body(): pl.pallas_call(store, out_shape=shapes, in_specs=[hbm] * 2, out_specs=(hb...  1.94 us

profile of v6, /device:TPU:1, one launch (start us, length us, event | category | flops | bytes accessed | tf_op | source)
XLA Modules:
  0.0 61.6 jit_solution(11389213690393894894)
XLA Ops:
  0.6 59.0 %shard_map.113 = (f32[3,1024]{1,0:T(4,128)}, f32[3,6,32,384]{3,2,1,0:T(8,128)}) custom-call(f32[3,6,32,384]{3,2,1,0:T(8,128)} %conc.1, f32[6,32,384]{2,1,0:T(8,128)} %u_in.1, f32[6,32,384]{2,1,0:T(8,128)} %v_in.1, f32[6,32,384]{2,1,0:T(8,128)} %k_in.1, f32[8,6]{1,0:T(8,128)} %kern_in.1, f32[3,1024]{1,0:T(4,128)} %observed_in.1, f32[1,1024]{1,0:T(1,128)} %bitcast.5, ...), custom_call_target="tpu_custom_call" | custom-call | tf_op jit(solution)/shard_map/pallas_call | solution.py:572
  59.7 1.9 %shard_map.114 = (f32[3,1024]{1,0:T(4,128)}, f32[3,6,32,384]{3,2,1,0:T(8,128)}) custom-call(f32[3,1024]{1,0:T(4,128)} %get-tuple-element.4.a, f32[3,6,32,384]{3,2,1,0:T(8,128)} %get-tuple-element.5.b), custom_call_target="tpu_custom_call" | custom-call | tf_op jit(solution)/shard_map/pallas_call | solution.py:628
